TPU v7x, 32 devices: a whole 2x2x4 slice. The times are simulated.
32 devices in a mesh: frames: 16 (over z, y, core), mp: 2 (over x).
Axes of the slice: x: 2, y: 2, z: 4, core: 2. Of those that a mesh axis runs over, the one named last changes fastest.
Arguments:
- latents: float32 [256, 1024], P('frames'), may hold values from -6 to 6
- noise: float32 [256, 1024], P('frames'), may hold values from -6 to 6
- levels: float32 [256], P('frames'), may hold values from 0.05 to 0.95
- clip_ids: int32 [256], replicated, may hold values from 0 to 7, never falling along the last dimension, each value on 1 to 64 neighbouring positions
- clean_flags: int32 [256], replicated, may hold values 0 or 1
- attn_weights: float32 [4, 1024, 1024], P(None, 'frames', 'mp')
- mlp_weights: float32 [2, 1024, 4096], P(None, 'frames', 'mp'), may hold values from -0.1875 to 0.1875
- mod_weight: float32 [1024, 6144], P('frames', 'mp'), may hold values from -0.1875 to 0.1875
- small_weights: float32 [1312, 1024], P(None, ('frames', 'mp'))
- attn_moment: float32 [4, 1024, 1024], P(None, 'frames', 'mp'), may hold values from -0.01171875 to 0.01171875
- mlp_moment: float32 [2, 1024, 4096], P(None, 'frames', 'mp'), may hold values from -0.01171875 to 0.01171875
- mod_moment: float32 [1024, 6144], P('frames', 'mp'), may hold values from -0.01171875 to 0.01171875
- small_moment: float32 [1312, 1024], P(None, ('frames', 'mp')), may hold values from -0.01171875 to 0.01171875
- attn_average: float32 [4, 1024, 1024], P(None, 'frames', 'mp'), may hold values from -0.1875 to 0.1875
- mlp_average: float32 [2, 1024, 4096], P(None, 'frames', 'mp'), may hold values from -0.1875 to 0.1875
- mod_average: float32 [1024, 6144], P('frames', 'mp'), may hold values from -0.1875 to 0.1875
- small_average: float32 [1312, 1024], P(None, ('frames', 'mp')), may hold values from -0.1875 to 0.1875
Outputs:
- loss_sum: float32 [], replicated
- noised_count: float32 [], replicated
- attn_new: float32 [4, 1024, 1024], P(None, 'frames', 'mp')
- attn_moment_new: float32 [4, 1024, 1024], P(None, 'frames', 'mp')
- attn_average_new: float32 [4, 1024, 1024], P(None, 'frames', 'mp')
- attn_copy: bfloat16 [4, 1024, 1024], P(None, 'frames', 'mp')
- mlp_new: float32 [2, 1024, 4096], P(None, 'frames', 'mp')
- mlp_moment_new: float32 [2, 1024, 4096], P(None, 'frames', 'mp')
- mlp_average_new: float32 [2, 1024, 4096], P(None, 'frames', 'mp')
- mlp_copy: bfloat16 [2, 1024, 4096], P(None, 'frames', 'mp')
- mod_new: float32 [1024, 6144], P('frames', 'mp')
- mod_moment_new: float32 [1024, 6144], P('frames', 'mp')
- mod_average_new: float32 [1024, 6144], P('frames', 'mp')
- mod_copy: bfloat16 [1024, 6144], P('frames', 'mp')
- small_new: float32 [1312, 1024], P(None, ('frames', 'mp'))
- small_moment_new: float32 [1312, 1024], P(None, ('frames', 'mp'))
- small_average_new: float32 [1312, 1024], P(None, ('frames', 'mp'))
- small_copy: bfloat16 [1312, 1024], P(None, ('frames', 'mp'))
Inputs may be any that keep to these rules, and one draw needn't show every extreme that they name: clip_ids never fall along the frames; each clip holds 1 to 64 frames, and some clip holds exactly 64.
All inputs are finite; a program needn't handle non-finite values.
Results may differ from a plain program's by a relative error of at most 0.0085.
Values may be sent and summed in bfloat16 or wider, within the bound.
A program may use at most 320 MiB of HBM per device.

v0:
```python
import functools
import math

import jax
import jax.numpy as jnp
import numpy as np
from jax import lax
from jax.experimental import pallas as pl
from jax.experimental.pallas import tpu as pltpu
from jax.sharding import PartitionSpec as P

D = 1024
HD = 64
CH = 4
FREQ = 256
GRID = 16
P_SIZE = 16
TPF = 64
REACH = 4


HIGH = lax.Precision.HIGHEST
EPSILON = 1e-06
MOMENTUM = 0.5
EMA_DECAY = 0.5
TP_AXIS = "mp"


def shifted(shard, axis, by):
    peers = lax.axis_size(axis)
    pairs = [(i, i + by) for i in range(peers) if 0 <= i + by < peers]
    return lax.ppermute(shard, axis, pairs)


def rotation_matrix(head_width):
    groups = [head_width // 4, 3 * head_width // 8, 3 * head_width // 8]
    rotation = np.zeros((head_width, head_width), np.float32)
    offset = 0
    for group_size in groups:
        half_size = group_size // 2
        for pair_index in range(half_size):
            rotation[offset + half_size + pair_index, offset + pair_index] = -1.0
            rotation[offset + pair_index, offset + half_size + pair_index] = 1.0
        offset += group_size
    return rotation


def rotary_angles(frame_pos, row_pos, col_pos, head_width):
    pieces = []
    for position, group_size in (
        (frame_pos, head_width // 4),
        (row_pos, 3 * head_width // 8),
        (col_pos, 3 * head_width // 8),
    ):
        half_size = group_size // 2
        frequency = 10000.0 ** (-jnp.arange(half_size, dtype=jnp.float32) / half_size)
        phases = position[:, None] * frequency[None, :]
        pieces += [phases, phases]
    return jnp.concatenate(pieces, axis=1)


def clip_positions(clip_ids):
    frame_index = jnp.arange(clip_ids.shape[0], dtype=jnp.int32)
    starts_here = jnp.concatenate([jnp.ones((1,), bool), clip_ids[1:] != clip_ids[:-1]])
    clip_start = lax.cummax(jnp.where(starts_here, frame_index, 0), axis=0)
    return frame_index - clip_start


def patchify(frame_data):
    frame_total = frame_data.shape[0]
    patch_side = GRID // 2
    shaped = frame_data.reshape(frame_total, CH, patch_side, 2, patch_side, 2)
    return shaped.transpose(0, 2, 4, 1, 3, 5).reshape(frame_total * patch_side * patch_side, CH * 4)


def layer_norm(vector):
    row_mean = jnp.mean(vector, axis=-1, keepdims=True)
    centred = vector - row_mean
    variance = jnp.mean(centred * centred, axis=-1, keepdims=True)
    return centred * lax.rsqrt(variance + EPSILON)


def modulate_local(shaped, shift_rows, scale_rows):
    return layer_norm(shaped) * (1.0 + scale_rows) + shift_rows


def time_features(level_eff):
    half_size = FREQ // 2
    frequency = jnp.exp(-math.log(10000.0) * jnp.arange(half_size, dtype=jnp.float32) / half_size)
    phases = (level_eff * 1000.0)[:, None] * frequency[None, :]
    return jnp.concatenate([jnp.cos(phases), jnp.sin(phases)], axis=1)


NT=(((1,),(1,)),((),()))
NN=(((1,),(0,)),((),()))

def dotf(a,b,dims=NN):
    return lax.dot_general(a,b,dims,preferred_element_type=jnp.float32)

def split_pair(xT):
    r=lax.broadcasted_iota(jnp.int32,xT.shape,0)
    z=jnp.zeros_like(xT)
    return jnp.where(r<HD,xT,z), jnp.where(r<HD,z,xT)

def keep_of(t,TK,TQ,cs,qf):
    kf=lax.broadcasted_iota(jnp.int32,(TK,TQ),0)//TPF+t*(TK//TPF)
    return (kf>=cs)&(kf<=qf)

def fwd_kernel(lo_ref,mid_ref,hi_ref,q_ref,k_ref,v_ref,cs_ref,o_ref,lse_ref,vT,*,TQ,TK,W0,NQ):
    KS=k_ref.shape[0]
    def tr(i,_):
        s=pl.multiple_of(i*TK,TK)
        vT[:,pl.ds(s,TK)]=v_ref[pl.ds(s,TK),:].T
        return 0
    lax.fori_loop(lo_ref[0],KS//TK,tr,0)
    def qtile(j,_):
        qs=pl.multiple_of(j*TQ,TQ)
        qT=(q_ref[pl.ds(qs,TQ),:].T)*jnp.bfloat16(0.125)
        qA,qB=split_pair(qT)
        cs=cs_ref[0:1,pl.ds(qs,TQ)]
        qf=lax.broadcasted_iota(jnp.int32,(1,TQ),1)//TPF+(W0+j*(TQ//TPF))
        def step(t,carry,masked):
            ks=pl.multiple_of(t*TK,TK)
            kt=k_ref[pl.ds(ks,TK),:]
            out=[]
            if masked: keep=keep_of(t,TK,TQ,cs,qf)
            for h,(qh,(m,l,o)) in enumerate(zip((qA,qB),carry)):
                s=dotf(kt,qh)
                if masked: s=jnp.where(keep,s,-1e30)
                mn=jnp.maximum(m,jnp.max(s,axis=0,keepdims=True))
                a=jnp.exp(m-mn)
                p=jnp.exp(s-mn)
                l=l*a+jnp.sum(p,axis=0,keepdims=True)
                o=o*a+dotf(vT[h*HD:(h+1)*HD,pl.ds(ks,TK)],p.astype(jnp.bfloat16))
                out.append((mn,l,o))
            return tuple(out)
        init=tuple((jnp.full((1,TQ),-1e29,jnp.float32),jnp.zeros((1,TQ),jnp.float32),jnp.zeros((HD,TQ),jnp.float32)) for _ in range(2))
        c=lax.fori_loop(lo_ref[j],mid_ref[j],lambda t,c:step(t,c,True),init)
        c=lax.fori_loop(mid_ref[j],hi_ref[j],lambda t,c:step(t,c,False),c)
        c=lax.fori_loop(hi_ref[j],(W0*TPF+(j+1)*TQ+TK-1)//TK,lambda t,c:step(t,c,True),c)
        oT=jnp.concatenate([c[0][2]/c[0][1],c[1][2]/c[1][1]],axis=0)
        o_ref[pl.ds(qs,TQ),:]=oT.T.astype(o_ref.dtype)
        lse_ref[0,0:1,pl.ds(qs,TQ)]=c[0][0]+jnp.log(c[0][1])
        lse_ref[0,1:2,pl.ds(qs,TQ)]=c[1][0]+jnp.log(c[1][1])
        return 0
    lax.fori_loop(0,NQ,qtile,0)

def tile_bounds(cs_rel,TQ,TK,W0,NQ):
    fq=TQ//TPF; fk=TK//TPF
    j=jnp.arange(NQ)
    first=cs_rel[::fq]; last=cs_rel[fq-1::fq]
    lo=first//fk
    dg=(W0+j*fq+1)//fk
    mid=jnp.minimum((last+fk-1)//fk,dg)
    mid=jnp.maximum(mid,lo)
    hi=jnp.maximum(dg,mid)
    return lo.astype(jnp.int32),mid.astype(jnp.int32),hi.astype(jnp.int32)

def attn_fwd(q,k,v,cs_rel,TQ=512,TK=512):
    T,Wd=q.shape; KS=k.shape[0]; P=Wd//128
    W0=(KS-T)//TPF; NQ=T//TQ
    lo,mid,hi=tile_bounds(cs_rel,TQ,TK,W0,NQ)
    cs_tok=jnp.broadcast_to(jnp.repeat(cs_rel,TPF)[None,:],(8,T)).astype(jnp.int32)
    return pl.pallas_call(
        functools.partial(fwd_kernel,TQ=TQ,TK=TK,W0=W0,NQ=NQ),
        grid_spec=pltpu.PrefetchScalarGridSpec(num_scalar_prefetch=3,grid=(P,),
            in_specs=[pl.BlockSpec((T,128),lambda p,*_:(0,p)),pl.BlockSpec((KS,128),lambda p,*_:(0,p)),pl.BlockSpec((KS,128),lambda p,*_:(0,p)),pl.BlockSpec((8,T),lambda p,*_:(0,0))],
            out_specs=[pl.BlockSpec((T,128),lambda p,*_:(0,p)),pl.BlockSpec((1,8,T),lambda p,*_:(p,0,0))],
            scratch_shapes=[pltpu.VMEM((128,KS),jnp.bfloat16)]),
        out_shape=[jax.ShapeDtypeStruct((T,Wd),jnp.float32),jax.ShapeDtypeStruct((P,8,T),jnp.float32)],
        compiler_params=pltpu.CompilerParams(vmem_limit_bytes=48<<20),
        cost_estimate=pl.CostEstimate(flops=10**11,bytes_accessed=2*10**7,transcendentals=3*10**7),
        name="attn_forward",
    )(lo,mid,hi,q,k,v,cs_tok)

def bwd_kernel(lo_ref,mid_ref,hi_ref,q_ref,k_ref,v_ref,do_ref,o_ref,lse_ref,cs_ref,dq_ref,dk_ref,dv_ref,kT,dkT,dvT,*,TQ,TK,W0,NQ):
    KS=k_ref.shape[0]
    def tr(i,_):
        s=pl.multiple_of(i*TK,TK)
        kT[:,pl.ds(s,TK)]=k_ref[pl.ds(s,TK),:].T
        return 0
    lax.fori_loop(lo_ref[0],KS//TK,tr,0)
    dkT[...]=jnp.zeros_like(dkT); dvT[...]=jnp.zeros_like(dvT)
    def qtile(j,_):
        qs=pl.multiple_of(j*TQ,TQ)
        qT=(q_ref[pl.ds(qs,TQ),:].T)*jnp.bfloat16(0.125)
        qh=split_pair(qT)
        doT=do_ref[pl.ds(qs,TQ),:].T
        doh=split_pair(doT)
        oT=o_ref[pl.ds(qs,TQ),:].T
        prod=oT*doT.astype(jnp.float32)
        delta=(jnp.sum(prod[:HD],axis=0,keepdims=True),jnp.sum(prod[HD:],axis=0,keepdims=True))
        lse=(lse_ref[0,0:1,pl.ds(qs,TQ)],lse_ref[0,1:2,pl.ds(qs,TQ)])
        cs=cs_ref[0:1,pl.ds(qs,TQ)]
        qf=lax.broadcasted_iota(jnp.int32,(1,TQ),1)//TPF+(W0+j*(TQ//TPF))
        def step(t,carry,masked):
            ks=pl.multiple_of(t*TK,TK)
            kt=k_ref[pl.ds(ks,TK),:]; vt=v_ref[pl.ds(ks,TK),:]
            out=[]
            if masked: keep=keep_of(t,TK,TQ,cs,qf)
            for h in range(2):
                r=slice(h*HD,(h+1)*HD)
                s=dotf(kt,qh[h])
                p=jnp.exp(s-lse[h])
                if masked: p=jnp.where(keep,p,0.0)
                dp=dotf(vt,doh[h])
                ds=(p*(dp-delta[h])).astype(jnp.bfloat16)
                pb=p.astype(jnp.bfloat16)
                dvT[r,pl.ds(ks,TK)]+=dotf(doT[r],pb,NT)
                dkT[r,pl.ds(ks,TK)]+=dotf(qT[r],ds,NT)
                out.append(carry[h]+dotf(kT[r,pl.ds(ks,TK)],ds))
            return tuple(out)
        init=(jnp.zeros((HD,TQ),jnp.float32),)*2
        c=lax.fori_loop(lo_ref[j],mid_ref[j],lambda t,c:step(t,c,True),init)
        c=lax.fori_loop(mid_ref[j],hi_ref[j],lambda t,c:step(t,c,False),c)
        c=lax.fori_loop(hi_ref[j],(W0*TPF+(j+1)*TQ+TK-1)//TK,lambda t,c:step(t,c,True),c)
        dq_ref[pl.ds(qs,TQ),:]=(jnp.concatenate(c,axis=0)*0.125).T
        return 0
    lax.fori_loop(0,NQ,qtile,0)
    def back(i,_):
        s=pl.multiple_of(i*TK,TK)
        dk_ref[pl.ds(s,TK),:]=dkT[:,pl.ds(s,TK)].T.astype(dk_ref.dtype)
        dv_ref[pl.ds(s,TK),:]=dvT[:,pl.ds(s,TK)].T.astype(dv_ref.dtype)
        return 0
    lax.fori_loop(0,KS//TK,back,0)

def attn_bwd(q,k,v,do,o,lse,cs_rel,TQ=512,TK=512,out_dt=jnp.bfloat16):
    T,Wd=q.shape; KS=k.shape[0]; P=Wd//128
    W0=(KS-T)//TPF; NQ=T//TQ
    lo,mid,hi=tile_bounds(cs_rel,TQ,TK,W0,NQ)
    cs_tok=jnp.broadcast_to(jnp.repeat(cs_rel,TPF)[None,:],(8,T)).astype(jnp.int32)
    tb=pl.BlockSpec((T,128),lambda p,*_:(0,p)); kb=pl.BlockSpec((KS,128),lambda p,*_:(0,p))
    return pl.pallas_call(
        functools.partial(bwd_kernel,TQ=TQ,TK=TK,W0=W0,NQ=NQ),
        grid_spec=pltpu.PrefetchScalarGridSpec(num_scalar_prefetch=3,grid=(P,),
            in_specs=[tb,kb,kb,tb,tb,pl.BlockSpec((1,8,T),lambda p,*_:(p,0,0)),pl.BlockSpec((8,T),lambda p,*_:(0,0))],
            out_specs=[tb,kb,kb],
            scratch_shapes=[pltpu.VMEM((128,KS),jnp.bfloat16),pltpu.VMEM((128,KS),jnp.float32),pltpu.VMEM((128,KS),jnp.float32)]),
        out_shape=[jax.ShapeDtypeStruct((T,Wd),jnp.float32),jax.ShapeDtypeStruct((KS,Wd),out_dt),jax.ShapeDtypeStruct((KS,Wd),out_dt)],
        compiler_params=pltpu.CompilerParams(vmem_limit_bytes=56<<20),
        cost_estimate=pl.CostEstimate(flops=2*10**11,bytes_accessed=5*10**7,transcendentals=3*10**7),
        name="attn_backward",
    )(lo,mid,hi,q,k,v,do,o,lse,cs_tok)


def update(weight, gradient, moment, average, learning_rate):
    moment_new = MOMENTUM * moment + gradient
    weight_new = weight - learning_rate * (gradient + MOMENTUM * moment_new)
    average_new = EMA_DECAY * average + (1.0 - EMA_DECAY) * weight_new
    return (weight_new, moment_new, average_new, weight_new.astype(jnp.bfloat16))


TN = (((0,), (0,)), ((), ()))


def norm_rows(v):
    centred = v - jnp.mean(v, axis=-1, keepdims=True)
    inverse = lax.rsqrt(jnp.mean(centred * centred, axis=-1, keepdims=True) + EPSILON)
    return centred * inverse, inverse


def norm_rows_back(grad, normed, inverse):
    return inverse * (
        grad
        - jnp.mean(grad, axis=-1, keepdims=True)
        - normed * jnp.mean(grad * normed, axis=-1, keepdims=True)
    )


def gelu_pair(x):
    c = math.sqrt(2.0 / math.pi)
    sq = x * x
    t = jnp.tanh(c * (x + 0.044715 * (x * sq)))
    half = 0.5 * (1.0 + t)
    return x * half, half + (0.5 * c) * x * (1.0 - t * t) * (1.0 + 0.134145 * sq)


def mid_kernel(
    o_ref, wo_ref, hid_ref, mod_ref, noise_ref, tw_ref, head_ref, gs_ref, wu_hbm, wd_hbm,
    dmix_ref, dx1_ref, dmod_ref, loss_ref, joint_hbm,
    wu_ref, wd_ref, att, x1, out, dx2, n2, n2t, act, dgl, dout, doutt, datt, datt_t,
    send_a, recv_a, send_c, recv_c, send_e, recv_e, stage, ghead_ref, go_ref, gh_t,
    wsem, gsem, ssem, rsem, *, tp,
):
    f = lax.axis_index("frames")
    h = lax.axis_index("mp")
    bf16 = jnp.bfloat16
    x_peer = {"mp": 1 - h}
    tp_peer = {"frames": f + 1 - 2 * lax.rem(f, 2)} if tp == "core" else x_peer
    half = hid_ref.shape[0]
    rows = 128
    chunks = half // rows
    width = hid_ref.shape[1]
    ff = wu_hbm.shape[1]
    e = o_ref.shape[1]
    ft = 512
    dt = 256

    weights = [
        pltpu.make_async_copy(wu_hbm, wu_ref, wsem.at[0]),
        pltpu.make_async_copy(wd_hbm, wd_ref, wsem.at[1]),
    ]
    for w in weights:
        w.start()

    barrier = pltpu.get_barrier_semaphore()
    pl.semaphore_signal(barrier, inc=1, device_id=x_peer, device_id_type=pl.DeviceIdType.MESH)
    if tp == "core":
        pl.semaphore_signal(barrier, inc=1, device_id=tp_peer, device_id_type=pl.DeviceIdType.MESH)
    pl.semaphore_wait(barrier, 2 if tp == "core" else 1)

    def at(start, size):
        return pl.ds(pl.multiple_of(start, size), size)

    def copy(src, dst, phase, c, peer):
        return pltpu.make_async_remote_copy(
            src_ref=src, dst_ref=dst, send_sem=ssem.at[phase, c], recv_sem=rsem.at[phase, c],
            device_id=peer, device_id_type=pl.DeviceIdType.MESH,
        )

    def copy_a(c):
        return copy(send_a.at[at(c * rows, rows)], recv_a.at[at(c * rows, rows)], 0, c, x_peer)

    def copy_b(c):
        return copy(
            n2.at[at(c * 2 * rows, rows)], n2.at[at(c * 2 * rows + rows, rows)], 1, c, tp_peer
        )

    def copy_c(c):
        return copy(send_c.at[at(c * rows, rows)], recv_c.at[at(c * rows, rows)], 2, c, tp_peer)

    def copy_d(c):
        return copy(
            dout.at[at(c * 2 * rows, rows)], dout.at[at(c * 2 * rows + rows, rows)], 3, c, tp_peer
        )

    def copy_e(c):
        return copy(send_e.at[at(c * rows, rows)], recv_e.at[at(c * rows, rows)], 4, c, tp_peer)

    def copy_f(c):
        mine = datt.at[at(h * half + c * rows, rows)]
        return copy(mine, mine, 5, c, x_peer)

    def phase_a(c, _):
        part = o_ref[at((1 - h) * half + c * rows, rows), :].astype(bf16)
        send_a[at(c * rows, rows), :] = dotf(part, wo_ref[...], NT).astype(bf16)
        copy_a(c).start()
        return 0

    lax.fori_loop(0, chunks, phase_a, 0)

    def phase_b(c, _):
        part = o_ref[at(h * half + c * rows, rows), :].astype(bf16)
        att[at(c * rows, rows), :] = dotf(part, wo_ref[...], NT)
        copy_a(c).wait_recv()
        for k in range(rows // TPF):
            r = at(c * rows + k * TPF, TPF)
            frame = pl.ds(c * (rows // TPF) + k, 1)
            a = att[r, :] + recv_a[r, :].astype(jnp.float32)
            att[r, :] = a
            v = hid_ref[r, :] + mod_ref[0, frame, :] * a
            x1[r, :] = v
            y, _inv = norm_rows(v)
            n2[at(c * 2 * rows + k * TPF, TPF), :] = (
                y * (1.0 + mod_ref[2, frame, :]) + mod_ref[1, frame, :]
            ).astype(bf16)
        copy_b(c).start()
        return 0

    lax.fori_loop(0, chunks, phase_b, 0)
    for w in weights:
        w.wait()

    def phase_c(c, _):
        copy_b(c).wait_recv()
        tok = at(c * 2 * rows, 2 * rows)
        n2t[:, tok] = n2[tok, :].T

        def up(i, _):
            cols = at(i * ft, ft)
            a, g = gelu_pair(dotf(n2[tok, :], wu_ref[:, cols]))
            act[tok, cols] = a.astype(bf16)
            dgl[tok, cols] = g.astype(bf16)
            return 0

        lax.fori_loop(0, ff // ft, up, 0)

        def down(i, _):
            cols = at(i * dt, dt)
            res = dotf(act[tok, :], wd_ref[cols, :], NT)
            out[at(c * rows, rows), cols] = res[:rows]
            send_c[at(c * rows, rows), cols] = res[rows:].astype(bf16)
            return 0

        lax.fori_loop(0, width // dt, down, 0)
        copy_c(c).start()
        return 0

    lax.fori_loop(0, chunks, phase_c, 0)

    ghead_ref[...] = jnp.zeros_like(ghead_ref)
    loss_ref[...] = jnp.zeros_like(loss_ref)

    def phase_d(c, _):
        copy_c(c).wait_recv()
        for k in range(rows // TPF):
            r = at(c * rows + k * TPF, TPF)
            frame = pl.ds(c * (rows // TPF) + k, 1)
            o = out[r, :] + recv_c[r, :].astype(jnp.float32)
            gate = mod_ref[3, frame, :]
            y, inv = norm_rows(x1[r, :] + gate * o)
            fn = y.astype(bf16)
            misfit = dotf(fn, head_ref[...], NT) - noise_ref[r, :]
            weighted = tw_ref[r, :] * misfit
            loss_ref[...] += weighted * misfit
            d_pred = (2.0 * gs_ref[0] * weighted).astype(bf16)
            ghead_ref[...] += dotf(d_pred, fn, TN)
            d_x2 = norm_rows_back(dotf(d_pred, head_ref[...]), y, inv)
            dx2[r, :] = d_x2
            dmod_ref[3, frame, :] = jnp.sum(d_x2 * o, axis=0, keepdims=True)
            dout[at(c * 2 * rows + k * TPF, TPF), :] = (gate * d_x2).astype(bf16)
        copy_d(c).start()
        return 0

    lax.fori_loop(0, chunks, phase_d, 0)

    def phase_e(c, _):
        copy_d(c).wait_recv()
        tok = at(c * 2 * rows, 2 * rows)
        doutt[:, tok] = dout[tok, :].T

        def down(i, _):
            cols = at(i * ft, ft)
            g = dotf(dout[tok, :], wd_ref[:, cols]) * dgl[tok, cols].astype(jnp.float32)
            dgl[tok, cols] = g.astype(bf16)
            return 0

        lax.fori_loop(0, ff // ft, down, 0)

        def up(i, _):
            cols = at(i * dt, dt)
            res = dotf(dgl[tok, :], wu_ref[cols, :], NT)
            out[at(c * rows, rows), cols] = res[:rows]
            send_e[at(c * rows, rows), cols] = res[rows:].astype(bf16)
            return 0

        lax.fori_loop(0, width // dt, up, 0)
        copy_e(c).start()
        return 0

    lax.fori_loop(0, chunks, phase_e, 0)

    def phase_f(c, _):
        copy_e(c).wait_recv()
        for k in range(rows // TPF):
            r = at(c * rows + k * TPF, TPF)
            frame = pl.ds(c * (rows // TPF) + k, 1)
            g = out[r, :] + recv_e[r, :].astype(jnp.float32)
            y, inv = norm_rows(x1[r, :])
            dmod_ref[1, frame, :] = jnp.sum(g, axis=0, keepdims=True)
            dmod_ref[2, frame, :] = jnp.sum(g * y, axis=0, keepdims=True)
            d_x1 = dx2[r, :] + norm_rows_back(g * (1.0 + mod_ref[2, frame, :]), y, inv)
            dx1_ref[r, :] = d_x1
            dmod_ref[0, frame, :] = jnp.sum(d_x1 * att[r, :], axis=0, keepdims=True)
            datt[at(h * half + c * rows + k * TPF, TPF), :] = (mod_ref[0, frame, :] * d_x1).astype(
                bf16
            )
        copy_f(c).start()
        return 0

    lax.fori_loop(0, chunks, phase_f, 0)

    def put(slot, i):
        k = lax.div(i, width // dt)
        return pltpu.make_async_copy(
            stage.at[slot],
            joint_hbm.at[at(lax.rem(i, width // dt) * dt, dt), at(k * ff, ff)],
            gsem.at[slot],
        )

    def weight_grads(left, right, k):
        def tile(i, _):
            step = k * (width // dt) + i
            slot = lax.rem(step, 2)

            @pl.when(step >= 2)
            def _():
                put(slot, step - 2).wait()

            def cols_of(j, _):
                cols = at(j * ft, ft)
                stage[slot, :, cols] = dotf(left[at(i * dt, dt), :], right[:, cols]).astype(bf16)
                return 0

            lax.fori_loop(0, ff // ft, cols_of, 0)
            put(slot, step).start()
            return 0

        lax.fori_loop(0, width // dt, tile, 0)

    weight_grads(n2t, dgl, 0)
    weight_grads(doutt, act, 1)

    def own_mix(c, _):
        tok = at(h * half + c * rows, rows)
        datt_t[:, tok] = datt[tok, :].T
        dmix_ref[tok, :] = dotf(datt[tok, :], wo_ref[...]).astype(bf16)
        return 0

    lax.fori_loop(0, chunks, own_mix, 0)

    def phase_g(c, _):
        tok = at((1 - h) * half + c * rows, rows)
        theirs = datt.at[tok]
        copy(theirs, theirs, 5, c, x_peer).wait_recv()
        datt_t[:, tok] = datt[tok, :].T
        dmix_ref[tok, :] = dotf(datt[tok, :], wo_ref[...]).astype(bf16)
        return 0

    lax.fori_loop(0, chunks, phase_g, 0)

    def grad_out(i, _):
        d = at(i * dt, dt)
        go_ref[d, :] = dotf(datt_t[d, :], o_ref[...].astype(bf16)).astype(bf16)
        return 0

    lax.fori_loop(0, width // dt, grad_out, 0)
    gh_t[...] = ghead_ref[...].T.astype(bf16)
    ends = [
        pltpu.make_async_copy(go_ref, joint_hbm.at[:, pl.ds(2 * ff, e)], gsem.at[2]),
        pltpu.make_async_copy(gh_t, joint_hbm.at[:, pl.ds(2 * ff + e, 128)], gsem.at[3]),
    ]
    for one in ends:
        one.start()
    for one in ends:
        one.wait()
    last = 2 * (width // dt)
    put((last - 2) % 2, last - 2).wait()
    put((last - 1) % 2, last - 1).wait()

    def sent(c, _):
        for one in (copy_a, copy_b, copy_c, copy_d, copy_e, copy_f):
            one(c).wait_send()
        return 0

    lax.fori_loop(0, chunks, sent, 0)


def mid_block(o, wo, hid, mod, noise, tw, head, gs, wu, wd, tp, cid):
    tok, e = o.shape
    half, width = hid.shape
    ff = wu.shape[1]
    own_frames = half // TPF
    f32, bf16 = jnp.float32, jnp.bfloat16
    vm = pl.BlockSpec(memory_space=pltpu.VMEM)
    anym = pl.BlockSpec(memory_space=pl.ANY)
    V = pltpu.VMEM
    return pl.pallas_call(
        functools.partial(mid_kernel, tp=tp),
        in_specs=[vm] * 7 + [pl.BlockSpec(memory_space=pltpu.SMEM), anym, anym],
        out_specs=[vm] * 4 + [anym],
        out_shape=[
            jax.ShapeDtypeStruct((tok, e), bf16),
            jax.ShapeDtypeStruct((half, width), f32),
            jax.ShapeDtypeStruct((4, own_frames, width), f32),
            jax.ShapeDtypeStruct((TPF, 128), f32),
            jax.ShapeDtypeStruct((width, 2 * ff + e + 128), bf16),
        ],
        scratch_shapes=[
            V((width, ff), bf16), V((width, ff), bf16),
            V((half, width), f32), V((half, width), f32), V((half, width), f32),
            V((half, width), f32),
            V((2 * half, width), bf16), V((width, 2 * half), bf16),
            V((2 * half, ff), bf16), V((2 * half, ff), bf16),
            V((2 * half, width), bf16), V((width, 2 * half), bf16),
            V((tok, width), bf16), V((width, tok), bf16),
            V((half, width), bf16), V((half, width), bf16),
            V((half, width), bf16), V((half, width), bf16),
            V((half, width), bf16), V((half, width), bf16),
            V((2, 256, ff), bf16), V((128, width), f32), V((width, e), bf16),
            V((width, 128), bf16),
            pltpu.SemaphoreType.DMA((2,)), pltpu.SemaphoreType.DMA((4,)),
            pltpu.SemaphoreType.DMA((6, half // 128)), pltpu.SemaphoreType.DMA((6, half // 128)),
        ],
        compiler_params=pltpu.CompilerParams(
            vmem_limit_bytes=62 << 20, collective_id=cid, has_side_effects=True
        ),
        cost_estimate=pl.CostEstimate(
            flops=4 * 10**10, bytes_accessed=3 * 10**7, transcendentals=2 * 10**6
        ),
        name="feed_forward",
    )(o, wo, hid, mod, noise, tw, head, gs, wu, wd)


def split_three(v):
    high = v.astype(jnp.bfloat16)
    left = v - high.astype(jnp.float32)
    middle = left.astype(jnp.bfloat16)
    return high, middle, (left - middle.astype(jnp.float32)).astype(jnp.bfloat16)


def turn_back(g, cosine, sine, rot):
    parts = split_three(g * sine)
    return (g * cosine + sum(dotf(p, rot, NT) for p in parts)).astype(jnp.bfloat16)


def tail_kernel(
    dq_ref, n1_ref, w_ref, cos_ref, sin_ref, rot_ref, hid_ref, scale_ref, dx1_ref, inp_ref,
    dk_hbm, dv_hbm,
    gq_ref, gin_ref, dss_ref,
    own, near, yrecv, zrecv, n1t, dproj, send_x, recv_x, part,
    lsem, s_near, r_near, s_y, r_y, s_z, r_z, s_x, r_x,
):
    f = lax.axis_index("frames")
    h = lax.axis_index("mp")
    n = lax.axis_size("frames")
    core = lax.rem(f, 2)
    odd = lax.rem(lax.div(f, 2), 2)
    core_peer = {"frames": f + 1 - 2 * core}
    y_peer = {"frames": f + 2 - 4 * odd}
    before = {"frames": lax.rem(f - 4 + n, n)}
    after = {"frames": lax.rem(f + 4, n)}
    x_peer = {"mp": 1 - h}
    tok, e = dq_ref.shape
    width = n1_ref.shape[1]
    half = tok // 2
    rows = 256
    chunks = tok // rows
    f32, bf16 = jnp.float32, jnp.bfloat16
    MESH = pl.DeviceIdType.MESH
    sides = (dk_hbm, dv_hbm)

    def at(start, size):
        return pl.ds(pl.multiple_of(start, size), size)

    loads = [
        pltpu.make_async_copy(
            sides[s].at[pl.ds(b * tok, tok)], own.at[s, j], lsem.at[s, j]
        )
        for s in range(2)
        for j, b in enumerate((4, 2, 0))
    ]
    for one in loads:
        one.start()

    barrier = pltpu.get_barrier_semaphore()
    for peer in (core_peer, y_peer, x_peer):
        pl.semaphore_signal(barrier, inc=1, device_id=peer, device_id_type=MESH)

    @pl.when(f >= 4)
    def _():
        pl.semaphore_signal(barrier, inc=1, device_id=before, device_id_type=MESH)

    @pl.when(f + 4 < n)
    def _():
        pl.semaphore_signal(barrier, inc=1, device_id=after, device_id_type=MESH)

    pl.semaphore_wait(barrier, 3 + jnp.where(f >= 4, 1, 0) + jnp.where(f + 4 < n, 1, 0))

    def rows_of(i):
        return lax.rem(i + (chunks // 2) * (1 - h), chunks) * rows

    def remote(src, dst, send, recv, peer):
        return pltpu.make_async_remote_copy(
            src_ref=src, dst_ref=dst, send_sem=send, recv_sem=recv, device_id=peer,
            device_id_type=MESH,
        )

    def near_copy(i, s, j):
        b = (3, 1)[j]
        return remote(
            sides[s].at[at(b * tok + rows_of(i), rows)],
            near.at[s, j, at(rows_of(i), rows)],
            s_near.at[s, j, i], r_near.at[s, j, i], core_peer,
        )

    def y_copy(i, s):
        r = at(rows_of(i), rows)
        return remote(own.at[s, 1, r], yrecv.at[s, r], s_y.at[s, i], r_y.at[s, i], y_peer)

    def z_copy(i, s):
        r = at(rows_of(i), rows)
        return remote(own.at[s, 2, r], zrecv.at[s, r], s_z.at[s, i], r_z.at[s, i], before)

    def x_copy(i):
        r = at(i * rows, rows)
        return remote(send_x.at[r], recv_x.at[r], s_x.at[i], r_x.at[i], x_peer)

    def start_near(i, _):
        for s in range(2):
            for j in range(2):
                near_copy(i, s, j).start()
        return 0

    lax.fori_loop(0, chunks, start_near, 0)

    @pl.when(f + 4 >= n)
    def _():
        zrecv[...] = jnp.zeros_like(zrecv)

    for one in loads:
        one.wait()
    low_core = core == 0

    def combine(i, _):
        r = at(rows_of(i), rows)
        for s in range(2):
            for j in range(2):
                near_copy(i, s, j).wait_recv()
            n3 = near[s, 0, r, :].astype(f32)
            n1_ = near[s, 1, r, :].astype(f32)
            own[s, 1, r, :] = (
                own[s, 1, r, :].astype(f32) + jnp.where(low_core, n1_, n3)
            ).astype(bf16)
            y_copy(i, s).start()
            own[s, 2, r, :] = (
                own[s, 2, r, :].astype(f32) + jnp.where(low_core, 0.0, n1_)
            ).astype(bf16)

            @pl.when((odd == 0) & (f >= 4))
            def _():
                z_copy(i, s).start()

        return 0

    lax.fori_loop(0, chunks, combine, 0)

    def turned(g, r, k):
        for b in range(e // 256):
            cols = slice(b * 256, (b + 1) * 256)
            dproj[k, r, cols] = turn_back(
                g[:, cols], cos_ref[r, :], sin_ref[r, :], rot_ref[...]
            )

    def relay(i, _):
        r = at(rows_of(i), rows)
        turned(dq_ref[r, :], r, 0)
        n1t[:, r] = n1_ref[r, :].T

        @pl.when(odd == 1)
        def _():
            for s in range(2):
                y_copy(i, s).wait_recv()

                @pl.when(f >= 4)
                def _():
                    own[s, 2, r, :] = (
                        own[s, 2, r, :].astype(f32) + yrecv[s, r, :].astype(f32)
                    ).astype(bf16)
                    z_copy(i, s).start()

        return 0

    lax.fori_loop(0, chunks, relay, 0)

    def grads(k):
        def tile(i, _):
            d = at(i * 256, 256)
            gq_ref[k, d, :] = dotf(n1t[d, :], dproj[k]).astype(bf16)
            return 0

        lax.fori_loop(0, width // 256, tile, 0)

    grads(0)

    def finish(i, _):
        r = at(rows_of(i), rows)
        for s in range(2):

            @pl.when(odd == 0)
            def _():
                y_copy(i, s).wait_recv()

            @pl.when(f + 4 < n)
            def _():
                z_copy(i, s).wait_recv()

            total = (
                own[s, 0, r, :].astype(f32)
                + jnp.where(low_core, near[s, 0, r, :].astype(f32), 0.0)
                + jnp.where(odd == 0, yrecv[s, r, :].astype(f32), 0.0)
                + zrecv[s, r, :].astype(f32)
            )
            if s == 0:
                turned(total, r, 1)
            else:
                dproj[2, r, :] = total.astype(bf16)

        def cols_of(j, _):
            cols = at(j * 256, 256)
            res = sum(dotf(dproj[k, r, :], w_ref[k, cols, :], NT) for k in range(3))

            @pl.when(i < chunks // 2)
            def _():
                send_x[at(i * rows, rows), cols] = res.astype(bf16)

            @pl.when(i >= chunks // 2)
            def _():
                part[at((i - chunks // 2) * rows, rows), cols] = res

            return 0

        lax.fori_loop(0, width // 256, cols_of, 0)

        @pl.when(i < chunks // 2)
        def _():
            x_copy(i).start()

        return 0

    lax.fori_loop(0, chunks, finish, 0)
    grads(1)
    grads(2)
    gin_ref[...] = jnp.zeros_like(gin_ref)

    def norm_back(i, _):
        x_copy(i).wait_recv()
        for k in range(rows // TPF):
            r = at(i * rows + k * TPF, TPF)
            frame = pl.ds(i * (rows // TPF) + k, 1)
            g = part[r, :] + recv_x[r, :].astype(f32)
            y, inv = norm_rows(hid_ref[r, :])
            dss_ref[0, frame, :] = jnp.sum(g, axis=0, keepdims=True)
            dss_ref[1, frame, :] = jnp.sum(g * y, axis=0, keepdims=True)
            d_hid = dx1_ref[r, :] + norm_rows_back(g * (1.0 + scale_ref[frame, :]), y, inv)
            gin_ref[...] += dotf(inp_ref[r, :], d_hid.astype(bf16), TN)
        return 0

    lax.fori_loop(0, half // rows, norm_back, 0)

    def sent(i, _):
        for s in range(2):
            for j in range(2):
                near_copy(i, s, j).wait_send()
            y_copy(i, s).wait_send()

            @pl.when(f >= 4)
            def _():
                z_copy(i, s).wait_send()

        @pl.when(i < chunks // 2)
        def _():
            x_copy(i).wait_send()

        return 0

    lax.fori_loop(0, chunks, sent, 0)


def tail_block(dq, n1, w, cosine, sine, rot, hid, scale, dx1, inp, dk, dv, cid):
    tok, e = dq.shape
    width = n1.shape[1]
    half = tok // 2
    f32, bf16 = jnp.float32, jnp.bfloat16
    vm = pl.BlockSpec(memory_space=pltpu.VMEM)
    anym = pl.BlockSpec(memory_space=pl.ANY)
    V = pltpu.VMEM
    D_ = pltpu.SemaphoreType.DMA
    chunks = tok // 256
    return pl.pallas_call(
        tail_kernel,
        in_specs=[vm] * 10 + [anym] * 2,
        out_specs=[vm] * 3,
        out_shape=[
            jax.ShapeDtypeStruct((3, width, e), bf16),
            jax.ShapeDtypeStruct((128, width), f32),
            jax.ShapeDtypeStruct((2, half // TPF, width), f32),
        ],
        scratch_shapes=[
            V((2, 3, tok, e), bf16), V((2, 2, tok, e), bf16), V((2, tok, e), bf16),
            V((2, tok, e), bf16), V((width, tok), bf16), V((3, tok, e), bf16),
            V((half, width), bf16), V((half, width), bf16), V((half, width), f32),
            D_((2, 3)), D_((2, 2, chunks)), D_((2, 2, chunks)), D_((2, chunks)), D_((2, chunks)),
            D_((2, chunks)), D_((2, chunks)), D_((chunks // 2,)), D_((chunks // 2,)),
        ],
        compiler_params=pltpu.CompilerParams(
            vmem_limit_bytes=56 << 20, collective_id=cid, has_side_effects=True
        ),
        cost_estimate=pl.CostEstimate(
            flops=2 * 10**10, bytes_accessed=3 * 10**7, transcendentals=0
        ),
        name="projection_backward",
    )(dq, n1, w, cosine, sine, rot, hid, scale, dx1, inp, dk, dv)


def per_device(
    latents,
    noise,
    levels,
    clip_ids,
    clean_flags,
    attn_weights,
    mlp_weights,
    mod_weight,
    small_weights,
    attn_moment,
    mlp_moment,
    mod_moment,
    small_moment,
    attn_average,
    mlp_average,
    mod_average,
    small_average,
):
    frame_count = latents.shape[0]
    tok_count = frame_count * TPF
    patch_side = GRID // 2
    frames_total = clip_ids.shape[0]
    tokens_total = frames_total * TPF
    width_local = attn_weights.shape[2]
    heads_local = width_local // HD
    key_span = (REACH + 1) * tok_count
    device = lax.axis_index("frames")
    mp_index = lax.axis_index("mp")
    first_frame = device * frame_count
    scale_qk = HD ** (-0.5)
    w_attn = lax.all_gather(attn_weights.astype(jnp.bfloat16), "frames", axis=1, tiled=True)
    w_mlp = lax.all_gather(mlp_weights.astype(jnp.bfloat16), "frames", axis=1, tiled=True)
    low_mod = mod_weight.astype(jnp.bfloat16)
    w_mod = lax.all_gather(low_mod, "frames", axis=0, tiled=True)
    small_low = lax.all_gather(
        small_weights.astype(jnp.bfloat16), ("frames", "mp"), axis=1, tiled=True
    )
    levels_all = lax.all_gather(levels, "frames", axis=0, tiled=True)
    small_full = small_low.astype(jnp.float32)
    noised_all = (1 - clean_flags).astype(jnp.float32)
    noised_count = jnp.sum(noised_all)
    noised = lax.dynamic_slice_in_dim(noised_all, first_frame, frame_count)
    level_eff = levels * noised
    signal_scale = jnp.repeat(jnp.cos(0.5 * math.pi * level_eff), TPF)
    noise_scale = jnp.repeat(jnp.sin(0.5 * math.pi * level_eff), TPF)
    noise_patches = patchify(noise)
    inputs = signal_scale[:, None] * patchify(latents) + noise_scale[:, None] * noise_patches
    in_clip_all = clip_positions(clip_ids)
    in_clip = jnp.repeat(
        lax.dynamic_slice_in_dim(in_clip_all, first_frame, frame_count), TPF
    ).astype(jnp.float32)
    within = jnp.arange(tok_count, dtype=jnp.int32) % TPF
    angles = rotary_angles(
        in_clip,
        (within // patch_side).astype(jnp.float32),
        (within % patch_side).astype(jnp.float32),
        HD,
    )
    cosine_table = jnp.tile(jnp.cos(angles), (1, heads_local))
    sine_table = jnp.tile(jnp.sin(angles), (1, heads_local))
    rotation = jnp.asarray(
        np.kron(np.eye(heads_local, dtype=np.float32), rotation_matrix(HD)), jnp.bfloat16
    )
    turn_four = jnp.asarray(np.kron(np.eye(4, dtype=np.float32), rotation_matrix(HD)), jnp.bfloat16)
    clip_start = (
        lax.dynamic_slice_in_dim(
            jnp.arange(frames_total, dtype=jnp.int32) - in_clip_all, first_frame, frame_count
        )
        - first_frame
        + REACH * frame_count
    )
    features_all = time_features(levels_all * noised_all)
    pre_one = jnp.dot(features_all, small_full[:FREQ], precision=HIGH)
    first_all = jax.nn.silu(pre_one)
    pre_two = jnp.dot(first_all, small_full[FREQ : FREQ + D], precision=HIGH)
    conditioning_all = jax.nn.silu(pre_two)
    conditioning = lax.dynamic_slice_in_dim(conditioning_all, first_frame, frame_count)
    mod_full = w_mod.astype(jnp.float32)
    modulation = lax.all_gather(
        jnp.dot(conditioning, mod_full, precision=HIGH), "mp", axis=1, tiled=True
    )
    pieces = [
        modulation[:, None, piece_index * D : (piece_index + 1) * D] for piece_index in range(6)
    ]
    shift_one, scale_one, gate_one, shift_two, scale_two, gate_two = pieces
    w_in = small_low[FREQ + D : FREQ + D + P_SIZE]
    w_head = small_low[FREQ + D + P_SIZE :]
    inputs_low = inputs.astype(jnp.bfloat16)
    shaped_zero = jnp.dot(inputs_low, w_in, preferred_element_type=jnp.float32).reshape(
        frame_count, TPF, D
    )
    normed_one = (
        modulate_local(shaped_zero, shift_one, scale_one).reshape(tok_count, D).astype(jnp.bfloat16)
    )
    turned_weights = jnp.einsum(
        "kde,ef->kdf", w_attn[:2], rotation, preferred_element_type=jnp.bfloat16
    )
    projected = jnp.einsum(
        "td,kde->kte", normed_one, w_attn[:3], preferred_element_type=jnp.float32
    )
    turned = jnp.einsum(
        "td,kde->kte", normed_one, turned_weights, preferred_element_type=jnp.float32
    )
    queries = (projected[0] * cosine_table + turned[0] * sine_table).astype(jnp.bfloat16)
    keys_own = (projected[1] * cosine_table + turned[1] * sine_table).astype(jnp.bfloat16)
    values_own = projected[2].astype(jnp.bfloat16)
    key_parts = [keys_own]
    value_parts = [values_own]
    for reach_step in range(1, REACH + 1):
        far_keys, far_values = shifted((keys_own, values_own), "frames", reach_step)
        key_parts.insert(0, far_keys)
        value_parts.insert(0, far_values)
    keys_wide = jnp.concatenate(key_parts, axis=0)
    values_wide = jnp.concatenate(value_parts, axis=0)

    heads_wide, log_totals = attn_fwd(queries, keys_wide, values_wide, clip_start)
    half = tok_count // 2
    own_frames = frame_count // 2

    def half_of(array, dim=0):
        size = array.shape[dim] // 2
        return lax.dynamic_slice_in_dim(array, mp_index * size, size, dim)

    token_weight = jnp.repeat(noised, TPF) / (TPF * P_SIZE)
    grad_scale = 1.0 / jnp.maximum(noised_count, 1.0)
    padding = ((0, 0), (0, 128 - P_SIZE))
    mod_mid = jnp.stack(
        [half_of(piece[:, 0]) for piece in (gate_one, shift_two, scale_two, gate_two)]
    )
    d_mixed, d_shaped_one, d_mod_mid, loss_parts, grad_joint = mid_block(
        heads_wide,
        w_attn[3],
        half_of(shaped_zero.reshape(tok_count, D)),
        mod_mid,
        jnp.pad(half_of(noise_patches), padding),
        jnp.broadcast_to(half_of(token_weight)[:, None], (half, 128)),
        jnp.pad(w_head, ((0, 128 - P_SIZE), (0, 0))),
        grad_scale.reshape(1),
        w_mlp[0],
        w_mlp[1],
        TP_AXIS,
        0,
    )
    loss_own = jnp.sum(loss_parts)
    sum_joint = lax.psum_scatter(grad_joint, "frames", scatter_dimension=0, tiled=True)
    d_queries, keys_grad_wide, values_grad_wide = attn_bwd(
        queries, keys_wide, values_wide, d_mixed, heads_wide, log_totals, clip_start
    )
    d_queries, sum_joint = lax.optimization_barrier((d_queries, sum_joint))
    grad_qkv, grad_in, d_first_mods = tail_block(
        d_queries,
        normed_one,
        w_attn[:3],
        cosine_table[:, : 4 * HD],
        sine_table[:, : 4 * HD],
        turn_four,
        half_of(shaped_zero.reshape(tok_count, D)),
        half_of(scale_one[:, 0]),
        d_shaped_one,
        jnp.pad(half_of(inputs_low), padding),
        keys_grad_wide,
        values_grad_wide,
        1,
    )
    grad_in = grad_in[:P_SIZE]
    flip = [(0, 1), (1, 0)]
    first_cols = jnp.concatenate([d_first_mods[0], d_first_mods[1], d_mod_mid[0]], axis=1)
    later_cols = jnp.concatenate([d_mod_mid[1], d_mod_mid[2], d_mod_mid[3]], axis=1)
    kept_cols = jnp.where(mp_index == 0, first_cols, later_cols)
    their_cols = lax.ppermute(jnp.where(mp_index == 0, later_cols, first_cols), "mp", flip)
    d_mod_own = jnp.concatenate(
        [
            jnp.where(mp_index == 0, kept_cols, their_cols),
            jnp.where(mp_index == 0, their_cols, kept_cols),
        ],
        axis=0,
    )
    mod_rows = mod_weight.shape[0]
    small_cols = small_weights.shape[1]
    d_mod_all = lax.all_gather(d_mod_own, "frames", axis=0, tiled=True)
    cond_rows = lax.dynamic_slice_in_dim(conditioning_all, device * mod_rows, mod_rows, 1)
    sum_mod = jnp.einsum("fr,fc->rc", cond_rows, d_mod_all, precision=HIGH)
    d_cond_part = jnp.einsum("fc,rc->fr", d_mod_all, low_mod.astype(jnp.float32), precision=HIGH)
    loss_both = loss_own + lax.ppermute(loss_own, "mp", flip)
    loss_rows = jnp.broadcast_to(loss_both, (8, mod_rows))
    d_cond_rows = jnp.concatenate([d_cond_part + lax.ppermute(d_cond_part, "mp", flip), loss_rows], axis=0)
    d_cond_all = lax.all_gather(d_cond_rows, "frames", axis=1, tiled=True)
    loss_sum = jnp.sum(d_cond_all[frames_total]) / mod_rows
    d_pre_two = jax.vjp(jax.nn.silu, pre_two)[1](d_cond_all[:frames_total])[0]
    first_col = (device * lax.axis_size("mp") + mp_index) * small_cols

    def own(array):
        return lax.dynamic_slice_in_dim(array, first_col, small_cols, 1)

    grad_second = jnp.einsum("fi,fj->ij", first_all, own(d_pre_two), precision=HIGH)
    second_rows = lax.dynamic_slice_in_dim(small_full, FREQ + first_col, small_cols, 0)
    d_first = jnp.einsum("fk,jk->fj", d_pre_two, second_rows, precision=HIGH)
    d_pre_one = jax.vjp(jax.nn.silu, own(pre_one))[1](d_first)[0]
    grad_first = jnp.einsum("fi,fj->ij", features_all, d_pre_one, precision=HIGH)
    joined = jnp.concatenate(
        [
            part.astype(jnp.bfloat16)
            for part in (grad_qkv[0], grad_qkv[1], grad_qkv[2], grad_in.T)
        ],
        axis=1,
    )
    joined_sum = lax.psum_scatter(joined, "frames", scatter_dimension=0, tiled=True).astype(
        jnp.float32
    )
    ff_cols = mlp_weights.shape[2]
    sum_joint = sum_joint.astype(jnp.float32)
    sum_mlp = jnp.stack([sum_joint[:, :ff_cols], sum_joint[:, ff_cols : 2 * ff_cols]])
    sum_attn = jnp.stack(
        [joined_sum[:, k * width_local : (k + 1) * width_local] for k in range(3)]
        + [sum_joint[:, 2 * ff_cols : 2 * ff_cols + width_local]]
    )
    head_first = 2 * ff_cols + width_local
    ends = jnp.concatenate(
        [joined_sum[:, 3 * width_local :], sum_joint[:, head_first : head_first + P_SIZE]], axis=1
    ).T
    sum_ends = half_of(ends, 1) + lax.ppermute(
        lax.dynamic_slice_in_dim(ends, (1 - mp_index) * small_cols, small_cols, 1), "mp", flip
    )
    sum_small = jnp.concatenate([grad_first, grad_second, sum_ends], axis=0)
    learning_rate = 0.5 * math.sqrt(tokens_total * P_SIZE / D)
    attn_new, attn_moment_new, attn_average_new, attn_copy = update(
        attn_weights, sum_attn, attn_moment, attn_average, learning_rate
    )
    mlp_new, mlp_moment_new, mlp_average_new, mlp_copy = update(
        mlp_weights, sum_mlp, mlp_moment, mlp_average, learning_rate
    )
    mod_new, mod_moment_new, mod_average_new, mod_copy = update(
        mod_weight, sum_mod, mod_moment, mod_average, learning_rate
    )
    small_new, small_moment_new, small_average_new, small_copy = update(
        small_weights, sum_small, small_moment, small_average, learning_rate
    )
    return (
        loss_sum,
        noised_count,
        attn_new,
        attn_moment_new,
        attn_average_new,
        attn_copy,
        mlp_new,
        mlp_moment_new,
        mlp_average_new,
        mlp_copy,
        mod_new,
        mod_moment_new,
        mod_average_new,
        mod_copy,
        small_new,
        small_moment_new,
        small_average_new,
        small_copy,
    )


def solution(mesh):
    return jax.shard_map(
        per_device,
        mesh=mesh,
        in_specs=(
            P("frames", None),
            P("frames", None),
            P("frames"),
            P(),
            P(),
            P(None, "frames", "mp"),
            P(None, "frames", "mp"),
            P("frames", "mp"),
            P(None, ("frames", "mp")),
            P(None, "frames", "mp"),
            P(None, "frames", "mp"),
            P("frames", "mp"),
            P(None, ("frames", "mp")),
            P(None, "frames", "mp"),
            P(None, "frames", "mp"),
            P("frames", "mp"),
            P(None, ("frames", "mp")),
        ),
        out_specs=(
            P(),
            P(),
            P(None, "frames", "mp"),
            P(None, "frames", "mp"),
            P(None, "frames", "mp"),
            P(None, "frames", "mp"),
            P(None, "frames", "mp"),
            P(None, "frames", "mp"),
            P(None, "frames", "mp"),
            P(None, "frames", "mp"),
            P("frames", "mp"),
            P("frames", "mp"),
            P("frames", "mp"),
            P("frames", "mp"),
            P(None, ("frames", "mp")),
            P(None, ("frames", "mp")),
            P(None, ("frames", "mp")),
            P(None, ("frames", "mp")),
        ),
        check_vma=False,
    )
```

profile of v0, /device:TPU:0, one launch (start us, length us, event | category | flops | bytes accessed | tf_op | source)
XLA Modules:
  0.0 1019.0 jit_solution(5757375611228936147)
XLA Ops:
  18.3 35.1 %all-reduce.4 = f32[256]{0:T(256)S(1)} all-reduce(f32[256]{0:T(256)S(1)} %dynamic-update-slice), channel_id=1, replica_groups=mesh['frames'=16,'mp'=2] {'frames'}, use_global_device_ids=true, to_apply=%add.4 | all-reduce | flops 256 | bytes 2048
  81.2 5.4 copy.98
  94.4 41.9 %all-gather.9.cloned.1.call-done = bf16[1024,3072]{1,0:T(8,128)(2,1)} async-done(((bf16[64,3072]{1,0:T(8,128)(2,1)}), bf16[1024,3072]{1,0:T(8,128)(2,1)}) %all-gather.9.cloned.1.call-update) | async-done | bytes 6291472 | tf_op jit(solution)/shard_map/all_gather | solution.py:920
  136.4 4.7 fusion.37
  141.1 8.2 all_gather.27
  152.0 36.4 %all-gather.11.cloned.1.call-done = bf16[4,1024,512]{2,1,0:T(8,128)(2,1)} async-done(((bf16[4,64,512]{2,1,0:T(8,128)(2,1)}), bf16[4,1024,512]{2,1,0:T(8,128)(2,1)}) %all-gather.11.cloned.1.call-update) | async-done | bytes 4194320 | tf_op jit(solution)/shard_map/all_gather | solution.py:917
  188.4 7.9 convolution_bitcast_fusion.1
  196.3 6.4 convolution_bitcast_fusion
  209.8 3.9 collective-permute-start.1
  233.4 5.6 collective-permute-done.2
  239.0 13.0 %collective-permute-start.5 = (bf16[1024,512]{1,0:T(8,128)(2,1)S(1)}, bf16[1024,512]{1,0:T(8,128)(2,1)S(1)}, u32[]{:S(2)}, u32[]{:S(2)}) collective-permute-start(bf16[1024,512]{1,0:T(8,128)(2,1)S(1)} %fusion.18), channel_id=1, source_target_pairs={{0,6},{2,8},{4,10},{6,12},{8,14},{10,16},{12,18},{14,20},{16,22},{... | collective-permute-start | bytes 3145736 | tf_op jit(solution)/shard_map/ppermute | solution.py:32
  252.7 24.4 %collective-permute-done.1 = bf16[1024,512]{1,0:T(8,128)(2,1)S(1)} collective-permute-done((bf16[1024,512]{1,0:T(8,128)(2,1)}, bf16[1024,512]{1,0:T(8,128)(2,1)S(1)}, u32[]{:S(2)}, u32[]{:S(2)}) %collective-permute-start.1) | collective-permute-done | bytes 1048608 | tf_op jit(solution)/shard_map/ppermute | solution.py:32
  277.1 19.2 %collective-permute-start.6 = (bf16[1024,512]{1,0:T(8,128)(2,1)S(1)}, bf16[1024,512]{1,0:T(8,128)(2,1)S(1)}, u32[]{:S(2)}, u32[]{:S(2)}) collective-permute-start(bf16[1024,512]{1,0:T(8,128)(2,1)S(1)} %fusion.18), channel_id=1, source_target_pairs={{0,4},{2,6},{4,8},{6,10},{8,12},{10,14},{12,16},{14,18},{16,20},{1... | collective-permute-start | bytes 3145736 | tf_op jit(solution)/shard_map/ppermute | solution.py:32
  301.5 16.5 %collective-permute-done.6 = bf16[1024,512]{1,0:T(8,128)(2,1)S(1)} collective-permute-done((bf16[1024,512]{1,0:T(8,128)(2,1)S(1)}, bf16[1024,512]{1,0:T(8,128)(2,1)S(1)}, u32[]{:S(2)}, u32[]{:S(2)}) %collective-permute-start.6) | collective-permute-done | bytes 1048608 | tf_op jit(solution)/shard_map/ppermute | solution.py:32
  322.3 21.4 %attn_forward.1 = (f32[1024,512]{1,0:T(8,128)S(1)}, f32[4,8,1024]{2,1,0:T(8,128)S(1)}) custom-call(s32[2]{0:T(128)S(1)} %get-tuple-element.64.lo_ref, s32[2]{0:T(128)S(1)} %get-tuple-element.63.mid_ref, s32[2]{0:T(128)S(1)} %get-tuple-element.62.hi_ref, bf16[1024,512]{1,0:T(8,128)(2,1)S(1)} %get-tuple-element.68.q_ref, bf16[5120,512]{1,0:T(8,128)(2,1)} %copy-done.35, ...), custom_call_target="tpu_custom_call" | custom-call | flops 99999997952 | bytes 20000000 | tf_op jit(solution)/shard_map/attn_forward/pallas_call | solution.py:164
  345.6 6.4 slice_bitcast_fusion
  352.8 133.5 %feed_forward.1 = (bf16[1024,512]{1,0:T(8,128)(2,1)}, f32[512,1024]{1,0:T(8,128)}, f32[4,8,1024]{2,1,0:T(8,128)}, f32[64,128]{1,0:T(8,128)}, bf16[1024,4736]{1,0:T(8,128)(2,1)}) custom-call(f32[1024,512]{1,0:T(8,128)} %copy-done.5, bf16[1024,512]{1,0:T(8,128)(2,1)} %slice_bitcast_fusion.6.wo_ref, f32[512,1024]{1,0:T(8,128)} %constant_dynamic-slice_fusion.4.hid_ref, ...), custom_call_target="tpu_custom_call" | custom-call | flops 40000000000 | bytes 30000000 | tf_op jit(solution)/shard_map/feed_forward/pallas_call | solution.py:558
  486.6 35.7 %attn_backward.1 = (f32[1024,512]{1,0:T(8,128)}, bf16[5120,512]{1,0:T(8,128)(2,1)}, bf16[5120,512]{1,0:T(8,128)(2,1)}) custom-call(s32[2]{0:T(128)} %copy-done.4, s32[2]{0:T(128)} %copy-done.3, s32[2]{0:T(128)} %copy-done.2, bf16[1024,512]{1,0:T(8,128)(2,1)} %copy-done, bf16[5120,512]{1,0:T(8,128)(2,1)} %copy-done.35, bf16[5120,512]{1,0:T(8,128)(2,1)} %copy-done.34, ...), custom_call_target="tpu_custom_call" | custom-call | flops 199999995904 | bytes 50000000 | tf_op jit(solution)/shard_map/attn_backward/pallas_call | solution.py:233
  522.3 216.7 %reduce-scatter.3.cloned.1.call-done = bf16[64,4736]{1,0:T(8,128)(2,1)} async-done(((bf16[1024,4736]{1,0:T(8,128)(2,1)}), bf16[64,4736]{1,0:T(8,128)(2,1)}) %reduce-scatter.3.cloned.1.call-update) | async-done | bytes 606224 | tf_op jit(solution)/shard_map/reduce_scatter | solution.py:1031
  739.0 76.6 %projection_backward.1 = (bf16[3,1024,512]{2,1,0:T(8,128)(2,1)}, f32[128,1024]{1,0:T(8,128)}, f32[2,8,1024]{2,1,0:T(8,128)}) custom-call(f32[1024,512]{1,0:T(8,128)} %get-tuple-element.38.dq_ref, bf16[1024,1024]{1,0:T(8,128)(2,1)} %fusion.n1_ref, bf16[3,1024,512]{2,1,0:T(8,128)(2,1)} %slice.203.w_ref, f32[1024,256]{1,0:T(8,128)} %slice.218.cos_ref, ...), custom_call_target="tpu_custom_call" | custom-call | flops 20000000000 | bytes 30000000 | tf_op jit(solution)/shard_map/projection_backward/pallas_call | solution.py:860
  840.1 65.2 %reduce-scatter.5.cloned.1.call-done = bf16[64,1552]{1,0:T(8,128)(2,1)} async-done(((bf16[1024,1552]{1,0:T(8,128)(2,1)}), bf16[64,1552]{1,0:T(8,128)(2,1)}) %reduce-scatter.5.cloned.1.call-update) | async-done | bytes 198672 | tf_op jit(solution)/shard_map/reduce_scatter | solution.py:1093
  906.7 45.9 %all-gather.15.cloned.1.call-done = f32[256,3072]{1,0:T(8,128)} async-done(((f32[16,3072]{1,0:T(8,128)}), f32[256,3072]{1,0:T(8,128)}) %all-gather.15.cloned.1.call-update) | async-done | bytes 3145744 | tf_op jit(solution)/shard_map/all_gather | solution.py:1066
  968.2 4.0 fusion.77
  974.1 26.2 %all-gather.17.cloned.1.call-done = f32[264,1024]{0,1:T(8,128)} async-done(((f32[264,64]{0,1:T(8,128)}), f32[264,1024]{0,1:T(8,128)}) %all-gather.17.cloned.1.call-update) | async-done | bytes 1081360 | tf_op jit(solution)/shard_map/all_gather | solution.py:1073
  (279 shorter events, 138.5 us)
Async XLA Ops:
  7.2 70.2 %all-gather.7.cloned.1.call-start = ((), (), s32[]{:S(2)}) async-start(), calls=%async_computation.2 | async-start | bytes 2973696 | tf_op jit(solution)/shard_map/all_gather | solution.py:921
  8.9 127.5 %all-gather.9.cloned.1.call-start = ((), (), s32[]{:S(2)}) async-start(), calls=%async_computation.3 | async-start | bytes 6684672 | tf_op jit(solution)/shard_map/all_gather | solution.py:920
  10.9 177.5 %all-gather.11.cloned.1.call-start = ((), (), s32[]{:S(2)}) async-start(), calls=%async_computation.4 | async-start | bytes 4456448 | tf_op jit(solution)/shard_map/all_gather | solution.py:917
  12.7 332.9 %all-gather.13.cloned.1.call-start = ((), (), s32[]{:S(2)}) async-start(), calls=%async_computation.5 | async-start | bytes 8912896 | tf_op jit(solution)/shard_map/all_gather | solution.py:918
  14.9 724.1 %reduce-scatter.3.cloned.1.call-start = ((), (), s32[]{:S(2)}) async-start(), calls=%async_computation.6 | async-start | bytes 10305536 | tf_op jit(solution)/shard_map/reduce_scatter | solution.py:1031
  75.1 244.8 %copy-start.2 = (s32[2]{0:T(128)}, s32[2]{0:T(128)S(1)}, u32[]{:S(2)}) copy-start(s32[2]{0:T(128)S(1)} %get-tuple-element.62.hi_ref) | copy-start | bytes 28
  75.2 244.8 %copy-start.3 = (s32[2]{0:T(128)}, s32[2]{0:T(128)S(1)}, u32[]{:S(2)}) copy-start(s32[2]{0:T(128)S(1)} %get-tuple-element.63.mid_ref) | copy-start | bytes 28
  75.2 244.8 %copy-start.4 = (s32[2]{0:T(128)}, s32[2]{0:T(128)S(1)}, u32[]{:S(2)}) copy-start(s32[2]{0:T(128)S(1)} %get-tuple-element.64.lo_ref) | copy-start | bytes 28
  206.5 32.5 %collective-permute-start.2 = (bf16[1024,512]{1,0:T(8,128)(2,1)}, bf16[1024,512]{1,0:T(8,128)(2,1)S(1)}, u32[]{:S(2)}, u32[]{:S(2)}) collective-permute-start(bf16[1024,512]{1,0:T(8,128)(2,1)} %get-tuple-element.67), channel_id=1, source_target_pairs={{0,4},{2,6},{4,8},{6,10},{8,12},{10,14},{12,16},{14,18},{16,20},{1... | collective-permute-start | bytes 3145736 | tf_op jit(solution)/shard_map/ppermute | solution.py:32
  209.8 67.3 %collective-permute-start.1 = (bf16[1024,512]{1,0:T(8,128)(2,1)}, bf16[1024,512]{1,0:T(8,128)(2,1)S(1)}, u32[]{:S(2)}, u32[]{:S(2)}) collective-permute-start(bf16[1024,512]{1,0:T(8,128)(2,1)} %get-tuple-element.67), channel_id=1, source_target_pairs={{0,6},{2,8},{4,10},{6,12},{8,14},{10,16},{12,18},{14,20},{16,22},{... | collective-permute-start | bytes 3145736 | tf_op jit(solution)/shard_map/ppermute | solution.py:32
  213.7 83.3 %collective-permute-start = (bf16[1024,512]{1,0:T(8,128)(2,1)}, bf16[1024,512]{1,0:T(8,128)(2,1)}, u32[]{:S(2)}, u32[]{:S(2)}) collective-permute-start(bf16[1024,512]{1,0:T(8,128)(2,1)} %get-tuple-element.67), channel_id=1, source_target_pairs={{0,8},{2,10},{4,12},{6,14},{8,16},{10,18},{12,20},{14,22},{16,24},... | collective-permute-start | bytes 3145736 | tf_op jit(solution)/shard_map/ppermute | solution.py:32
  228.6 71.3 %collective-permute-start.3 = (bf16[1024,512]{1,0:T(8,128)(2,1)}, bf16[1024,512]{1,0:T(8,128)(2,1)S(1)}, u32[]{:S(2)}, u32[]{:S(2)}) collective-permute-start(bf16[1024,512]{1,0:T(8,128)(2,1)} %get-tuple-element.67), channel_id=1, source_target_pairs={{0,2},{2,4},{4,6},{6,8},{8,10},{10,12},{12,14},{14,16},{16,18},{18... | collective-permute-start | bytes 3145736 | tf_op jit(solution)/shard_map/ppermute | solution.py:32
  231.7 69.6 %collective-permute-start.4 = (bf16[1024,512]{1,0:T(8,128)(2,1)S(1)}, bf16[1024,512]{1,0:T(8,128)(2,1)S(1)}, u32[]{:S(2)}, u32[]{:S(2)}) collective-permute-start(bf16[1024,512]{1,0:T(8,128)(2,1)S(1)} %fusion.18), channel_id=1, source_target_pairs={{0,8},{2,10},{4,12},{6,14},{8,16},{10,18},{12,20},{14,22},{16,24},... | collective-permute-start | bytes 3145736 | tf_op jit(solution)/shard_map/ppermute | solution.py:32
  239.0 62.5 %collective-permute-start.5 = (bf16[1024,512]{1,0:T(8,128)(2,1)S(1)}, bf16[1024,512]{1,0:T(8,128)(2,1)S(1)}, u32[]{:S(2)}, u32[]{:S(2)}) collective-permute-start(bf16[1024,512]{1,0:T(8,128)(2,1)S(1)} %fusion.18), channel_id=1, source_target_pairs={{0,6},{2,8},{4,10},{6,12},{8,14},{10,16},{12,18},{14,20},{16,22},{... | collective-permute-start | bytes 3145736 | tf_op jit(solution)/shard_map/ppermute | solution.py:32
  277.1 40.9 %collective-permute-start.6 = (bf16[1024,512]{1,0:T(8,128)(2,1)S(1)}, bf16[1024,512]{1,0:T(8,128)(2,1)S(1)}, u32[]{:S(2)}, u32[]{:S(2)}) collective-permute-start(bf16[1024,512]{1,0:T(8,128)(2,1)S(1)} %fusion.18), channel_id=1, source_target_pairs={{0,4},{2,6},{4,8},{6,10},{8,12},{10,14},{12,16},{14,18},{16,20},{1... | collective-permute-start | bytes 3145736 | tf_op jit(solution)/shard_map/ppermute | solution.py:32
  297.0 21.1 %collective-permute-start.7 = (bf16[1024,512]{1,0:T(8,128)(2,1)S(1)}, bf16[1024,512]{1,0:T(8,128)(2,1)S(1)}, u32[]{:S(2)}, u32[]{:S(2)}) collective-permute-start(bf16[1024,512]{1,0:T(8,128)(2,1)S(1)} %fusion.18), channel_id=1, source_target_pairs={{0,2},{2,4},{4,6},{6,8},{8,10},{10,12},{12,14},{14,16},{16,18},{18... | collective-permute-start | bytes 3145736 | tf_op jit(solution)/shard_map/ppermute | solution.py:32
  486.3 419.0 %reduce-scatter.5.cloned.1.call-start = ((), (), s32[]{:S(2)}) async-start(), calls=%async_computation.9 | async-start | bytes 3620864 | tf_op jit(solution)/shard_map/reduce_scatter | solution.py:1093
  820.7 131.9 %all-gather.15.cloned.1.call-start = ((), (), s32[]{:S(2)}) async-start(), calls=%async_computation.7 | async-start | bytes 3342336 | tf_op jit(solution)/shard_map/all_gather | solution.py:1066
  820.8 4.7 collective-permute-start.8
  826.2 174.1 %all-gather.17.cloned.1.call-start = ((), (), s32[]{:S(2)}) async-start(), calls=%async_computation.8 | async-start | bytes 1671168 | tf_op jit(solution)/shard_map/all_gather | solution.py:1073
  828.8 3.6 collective-permute-start.10
  835.3 117.3 %copy-start.15 = (bf16[64,3072]{1,0:T(8,128)(2,1)S(1)}, bf16[64,3072]{1,0:T(8,128)(2,1)}, u32[]{:S(2)}) copy-start(bf16[64,3072]{1,0:T(8,128)(2,1)} %convert_element_type.94) | copy-start | bytes 1179652
  956.4 4.6 collective-permute-start.9
  958.7 8.7 collective-permute-start.11
  (52 other events, 616.9 us)
Sparse Core Ops, SparseCore 0:
  11.5 61.4 all-gather.6
  75.8 60.4 all-gather.8
  139.1 49.2 all-gather.10
  191.0 102.9 all-gather.12
  486.5 252.5 reduce-scatter.2
  820.8 84.4 reduce-scatter.4
  908.5 44.0 all-gather.14
  961.8 38.4 all-gather.16
where the time goes:
time: 1020 us
  waiting for transfers between devices  485 us (48%)
  Pallas kernels  267 us (26%)
  local copies, waits for them, and re-layouts  71 us (7%)
  starting transfers between devices  52.6 us (5%)
  blocking collectives  43.3 us (4%)
  other arithmetic  42.6 us (4%)
  matrix products  37.6 us (4%)
  between operations  20.1 us (2%)
    reduce_scatter x1, waiting for transfers between devices, per_device(): lax.psum_scatter(grad_joint, 'frames', scatter_dimension=0, tiled=True)  217 us
    pallas_call x1, Pallas kernels, mid_block(): pl.pallas_call(functools.partial(mid_kernel, tp=tp), in_specs=[vm] * 7 +...  133 us
    pallas_call x1, Pallas kernels, tail_block(): pl.pallas_call(tail_kernel, in_specs=[vm] * 10 + [anym] * 2, out_specs=[v...  76.6 us
    reduce_scatter x1, waiting for transfers between devices, per_device(): lax.psum_scatter(joined, 'frames', scatter_dimension=0, tiled=True)  65.2 us
    ppermute x8, starting transfers between devices, shifted(): return lax.ppermute(shard, axis, pairs)  47 us
    ppermute x8, waiting for transfers between devices, shifted(): return lax.ppermute(shard, axis, pairs)  46.5 us
    all_gather x1, waiting for transfers between devices, per_device(): d_mod_all = lax.all_gather(d_mod_own, 'frames', axis=0, tiled=True)  45.9 us
    all_gather x1, waiting for transfers between devices, per_device(): w_mod = lax.all_gather(low_mod, 'frames', axis=0, tiled=True)  41.9 us
  transfers between devices with their start and end apart: 20, of which 11 were waited for; matrix products, arithmetic and copies ran while one was open for 11% of the time, Pallas kernels for 6%

commit v1 on v0

--- a/solution.py
+++ b/solution.py
@@ -24,12 +24,6 @@
 MOMENTUM = 0.5
 EMA_DECAY = 0.5
 TP_AXIS = "mp"
-
-
-def shifted(shard, axis, by):
-    peers = lax.axis_size(axis)
-    pairs = [(i, i + by) for i in range(peers) if 0 <= i + by < peers]
-    return lax.ppermute(shard, axis, pairs)
 
 
 def rotation_matrix(head_width):
@@ -277,7 +271,7 @@
 
 def mid_kernel(
     o_ref, wo_ref, hid_ref, mod_ref, noise_ref, tw_ref, head_ref, gs_ref, wu_hbm, wd_hbm,
-    dmix_ref, dx1_ref, dmod_ref, loss_ref, joint_hbm,
+    dmix_ref, dx1_ref, dmod_ref, loss_ref, up_hbm, rest_hbm,
     wu_ref, wd_ref, att, x1, out, dx2, n2, n2t, act, dgl, dout, doutt, datt, datt_t,
     send_a, recv_a, send_c, recv_c, send_e, recv_e, stage, ghead_ref, go_ref, gh_t,
     wsem, gsem, ssem, rsem, *, tp,
@@ -470,22 +464,18 @@
 
     lax.fori_loop(0, chunks, phase_f, 0)
 
-    def put(slot, i):
-        k = lax.div(i, width // dt)
-        return pltpu.make_async_copy(
-            stage.at[slot],
-            joint_hbm.at[at(lax.rem(i, width // dt) * dt, dt), at(k * ff, ff)],
-            gsem.at[slot],
-        )
-
-    def weight_grads(left, right, k):
+    def weight_grads(left, right, target):
+        def put(slot, i):
+            return pltpu.make_async_copy(
+                stage.at[slot], target.at[at(i * dt, dt), pl.ds(0, ff)], gsem.at[slot]
+            )
+
         def tile(i, _):
-            step = k * (width // dt) + i
-            slot = lax.rem(step, 2)
-
-            @pl.when(step >= 2)
-            def _():
-                put(slot, step - 2).wait()
+            slot = lax.rem(i, 2)
+
+            @pl.when(i >= 2)
+            def _():
+                put(slot, i - 2).wait()
 
             def cols_of(j, _):
                 cols = at(j * ft, ft)
@@ -493,13 +483,15 @@
                 return 0
 
             lax.fori_loop(0, ff // ft, cols_of, 0)
-            put(slot, step).start()
+            put(slot, i).start()
             return 0
 
         lax.fori_loop(0, width // dt, tile, 0)
-
-    weight_grads(n2t, dgl, 0)
-    weight_grads(doutt, act, 1)
+        for i in (width // dt - 2, width // dt - 1):
+            put(i % 2, i).wait()
+
+    weight_grads(n2t, dgl, up_hbm)
+    weight_grads(doutt, act, rest_hbm)
 
     def own_mix(c, _):
         tok = at(h * half + c * rows, rows)
@@ -527,17 +519,13 @@
     lax.fori_loop(0, width // dt, grad_out, 0)
     gh_t[...] = ghead_ref[...].T.astype(bf16)
     ends = [
-        pltpu.make_async_copy(go_ref, joint_hbm.at[:, pl.ds(2 * ff, e)], gsem.at[2]),
-        pltpu.make_async_copy(gh_t, joint_hbm.at[:, pl.ds(2 * ff + e, 128)], gsem.at[3]),
+        pltpu.make_async_copy(go_ref, rest_hbm.at[:, pl.ds(ff, e)], gsem.at[2]),
+        pltpu.make_async_copy(gh_t, rest_hbm.at[:, pl.ds(ff + e, 128)], gsem.at[3]),
     ]
     for one in ends:
         one.start()
     for one in ends:
         one.wait()
-    last = 2 * (width // dt)
-    put((last - 2) % 2, last - 2).wait()
-    put((last - 1) % 2, last - 1).wait()
-
     def sent(c, _):
         for one in (copy_a, copy_b, copy_c, copy_d, copy_e, copy_f):
             one(c).wait_send()
@@ -558,13 +546,14 @@
     return pl.pallas_call(
         functools.partial(mid_kernel, tp=tp),
         in_specs=[vm] * 7 + [pl.BlockSpec(memory_space=pltpu.SMEM), anym, anym],
-        out_specs=[vm] * 4 + [anym],
+        out_specs=[vm] * 4 + [anym] * 2,
         out_shape=[
             jax.ShapeDtypeStruct((tok, e), bf16),
             jax.ShapeDtypeStruct((half, width), f32),
             jax.ShapeDtypeStruct((4, own_frames, width), f32),
             jax.ShapeDtypeStruct((TPF, 128), f32),
-            jax.ShapeDtypeStruct((width, 2 * ff + e + 128), bf16),
+            jax.ShapeDtypeStruct((width, ff), bf16),
+            jax.ShapeDtypeStruct((width, ff + e + 128), bf16),
         ],
         scratch_shapes=[
             V((width, ff), bf16), V((width, ff), bf16),
@@ -881,6 +870,247 @@
         ),
         name="projection_backward",
     )(dq, n1, w, cosine, sine, rot, hid, scale, dx1, inp, dk, dv)
+
+
+def proj_kernel(
+    inp_ref, win_ref, mod_ref, w_ref, cos_ref, sin_ref, rot_ref,
+    n1_ref, hid_ref, q_ref, k_hbm, v_hbm,
+    kv, wr,
+    lsem, s_core, r_core, s_y, r_y, s_z, r_z,
+):
+    f = lax.axis_index("frames")
+    h = lax.axis_index("mp")
+    n = lax.axis_size("frames")
+    core = lax.rem(f, 2)
+    odd = lax.rem(lax.div(f, 2), 2)
+    core_peer = {"frames": f + 1 - 2 * core}
+    y_peer = {"frames": f + 2 - 4 * odd}
+    before = {"frames": lax.rem(f - 4 + n, n)}
+    after = {"frames": lax.rem(f + 4, n)}
+    tok, width = n1_ref.shape
+    e = q_ref.shape[1]
+    half = tok // 2
+    rows = 256
+    chunks = tok // rows
+    bf16 = jnp.bfloat16
+    MESH = pl.DeviceIdType.MESH
+    sides = (k_hbm, v_hbm)
+    has_z = f >= 4
+    has_next = f + 4 < n
+    has_y = has_z | (odd == 1)
+
+    def at(start, size):
+        return pl.ds(pl.multiple_of(start, size), size)
+
+    barrier = pltpu.get_barrier_semaphore()
+    for peer in (core_peer, y_peer):
+        pl.semaphore_signal(barrier, inc=1, device_id=peer, device_id_type=MESH)
+
+    @pl.when(has_z)
+    def _():
+        pl.semaphore_signal(barrier, inc=1, device_id=before, device_id_type=MESH)
+
+    @pl.when(has_next)
+    def _():
+        pl.semaphore_signal(barrier, inc=1, device_id=after, device_id_type=MESH)
+
+    def embed(i, _):
+        for k in range(2):
+            r = at(i * 2 * TPF + k * TPF, TPF)
+            frame = pl.ds(i * 2 + k, 1)
+            v = dotf(inp_ref[r, :], win_ref[...])
+            y, _inv = norm_rows(v)
+            n1_ref[r, :] = (y * (1.0 + mod_ref[1, frame, :]) + mod_ref[0, frame, :]).astype(bf16)
+
+            @pl.when(lax.div(i * 2 * TPF, half) == h)
+            def _():
+                hid_ref[at(lax.rem(i * 2 * TPF, half) + k * TPF, TPF), :] = v
+
+        return 0
+
+    lax.fori_loop(0, tok // (2 * TPF), embed, 0)
+
+    def turn_weights(i, _):
+        d = at(i * 256, 256)
+        for k in range(2):
+            for b in range(e // 256):
+                cols = slice(b * 256, (b + 1) * 256)
+                wr[k, d, cols] = dotf(w_ref[k, d, cols], rot_ref[...]).astype(bf16)
+        return 0
+
+    lax.fori_loop(0, width // 256, turn_weights, 0)
+    pl.semaphore_wait(barrier, 2 + jnp.where(has_z, 1, 0) + jnp.where(has_next, 1, 0))
+
+    def remote(src, dst, send, recv, peer):
+        return pltpu.make_async_remote_copy(
+            src_ref=src, dst_ref=dst, send_sem=send, recv_sem=recv, device_id=peer,
+            device_id_type=MESH,
+        )
+
+    def block(s, b, i):
+        return sides[s].at[at(b * tok + i * rows, rows)]
+
+    def mine(s, i):
+        return kv.at[s, at(i * rows, rows)]
+
+    def keep(s, i):
+        return pltpu.make_async_copy(mine(s, i), block(s, 4, i), lsem.at[s, i])
+
+    def z_copy(s, i):
+        return remote(mine(s, i), block(s, 0, i), s_z.at[s, i], r_z.at[s, i], after)
+
+    def y_copy(s, i, src):
+        return remote(src, block(s, 2, i), s_y.at[s, i], r_y.at[s, i], y_peer)
+
+    def core_copy(s, i, j, src):
+        return remote(
+            src, block(s, (3, 1)[j], i), s_core.at[j, s, i], r_core.at[j, s, i], core_peer
+        )
+
+    def rotated(r, k):
+        cosine, sine = cos_ref[r, :], sin_ref[r, :]
+        parts = []
+        for b in range(e // 256):
+            cols = slice(b * 256, (b + 1) * 256)
+            plain = dotf(n1_ref[r, :], w_ref[k, :, cols])
+            turned = dotf(n1_ref[r, :], wr[k, :, cols])
+            parts.append((plain * cosine + turned * sine).astype(bf16))
+        return parts
+
+    def own_chunk(i, _):
+        r = at(i * rows, rows)
+        for b, part in enumerate(rotated(r, 1)):
+            kv[0, r, b * 256 : (b + 1) * 256] = part
+        kv[1, r, :] = dotf(n1_ref[r, :], w_ref[2]).astype(bf16)
+        for s in range(2):
+            keep(s, i).start()
+
+            @pl.when(has_next)
+            def _():
+                z_copy(s, i).start()
+
+            @pl.when(odd == 0)
+            def _():
+                y_copy(s, i, mine(s, i)).start()
+
+            @pl.when(core == 0)
+            def _():
+                core_copy(s, i, 0, mine(s, i)).start()
+
+        return 0
+
+    lax.fori_loop(0, chunks, own_chunk, 0)
+
+    def queries(i, _):
+        r = at(i * rows, rows)
+        for b, part in enumerate(rotated(r, 0)):
+            q_ref[r, b * 256 : (b + 1) * 256] = part
+        return 0
+
+    lax.fori_loop(0, chunks, queries, 0)
+
+    def from_z(i, _):
+        @pl.when(has_z)
+        def _():
+            for s in range(2):
+                z_copy(s, i).wait_recv()
+
+                @pl.when(odd == 1)
+                def _():
+                    y_copy(s, i, block(s, 0, i)).start()
+
+                @pl.when(core == 1)
+                def _():
+                    core_copy(s, i, 1, block(s, 0, i)).start()
+
+        return 0
+
+    lax.fori_loop(0, chunks, from_z, 0)
+
+    def from_y(i, _):
+        @pl.when(has_y)
+        def _():
+            for s in range(2):
+                y_copy(s, i, mine(s, i)).wait_recv()
+
+                @pl.when(core == 1)
+                def _():
+                    core_copy(s, i, 0, block(s, 2, i)).start()
+
+                @pl.when(core == 0)
+                def _():
+                    core_copy(s, i, 1, block(s, 2, i)).start()
+
+        return 0
+
+    lax.fori_loop(0, chunks, from_y, 0)
+
+    def ended(i, _):
+        for s in range(2):
+            keep(s, i).wait()
+
+            @pl.when((core == 1) | has_y)
+            def _():
+                core_copy(s, i, 0, mine(s, i)).wait_recv()
+
+            @pl.when(((core == 1) & has_y) | has_z)
+            def _():
+                core_copy(s, i, 1, mine(s, i)).wait_recv()
+
+            @pl.when(has_next)
+            def _():
+                z_copy(s, i).wait_send()
+
+            @pl.when((odd == 0) | has_z)
+            def _():
+                y_copy(s, i, mine(s, i)).wait_send()
+
+            @pl.when((core == 0) | has_y)
+            def _():
+                core_copy(s, i, 0, mine(s, i)).wait_send()
+
+            @pl.when(((core == 0) & has_y) | has_z)
+            def _():
+                core_copy(s, i, 1, mine(s, i)).wait_send()
+
+        return 0
+
+    lax.fori_loop(0, chunks, ended, 0)
+
+
+def proj_block(inp, win, mod, w, cosine, sine, rot, reach, cid):
+    tok = inp.shape[0]
+    width, e = w.shape[1:]
+    f32, bf16 = jnp.float32, jnp.bfloat16
+    vm = pl.BlockSpec(memory_space=pltpu.VMEM)
+    anym = pl.BlockSpec(memory_space=pl.ANY)
+    V = pltpu.VMEM
+    D_ = pltpu.SemaphoreType.DMA
+    chunks = tok // 256
+    return pl.pallas_call(
+        proj_kernel,
+        in_specs=[vm] * 7,
+        out_specs=[vm] * 3 + [anym] * 2,
+        out_shape=[
+            jax.ShapeDtypeStruct((tok, width), bf16),
+            jax.ShapeDtypeStruct((tok // 2, width), f32),
+            jax.ShapeDtypeStruct((tok, e), bf16),
+            jax.ShapeDtypeStruct(((reach + 1) * tok, e), bf16),
+            jax.ShapeDtypeStruct(((reach + 1) * tok, e), bf16),
+        ],
+        scratch_shapes=[
+            V((2, tok, e), bf16), V((2, width, e), bf16),
+            D_((2, chunks)), D_((2, 2, chunks)), D_((2, 2, chunks)), D_((2, chunks)),
+            D_((2, chunks)), D_((2, chunks)), D_((2, chunks)),
+        ],
+        compiler_params=pltpu.CompilerParams(
+            vmem_limit_bytes=48 << 20, collective_id=cid, has_side_effects=True
+        ),
+        cost_estimate=pl.CostEstimate(
+            flops=6 * 10**10, bytes_accessed=3 * 10**7, transcendentals=0
+        ),
+        name="projection_forward",
+    )(inp, win, mod, w, cosine, sine, rot)
 
 
 def per_device(
@@ -942,11 +1172,8 @@
         (within % patch_side).astype(jnp.float32),
         HD,
     )
-    cosine_table = jnp.tile(jnp.cos(angles), (1, heads_local))
-    sine_table = jnp.tile(jnp.sin(angles), (1, heads_local))
-    rotation = jnp.asarray(
-        np.kron(np.eye(heads_local, dtype=np.float32), rotation_matrix(HD)), jnp.bfloat16
-    )
+    cosine_table = jnp.tile(jnp.cos(angles), (1, 4))
+    sine_table = jnp.tile(jnp.sin(angles), (1, 4))
     turn_four = jnp.asarray(np.kron(np.eye(4, dtype=np.float32), rotation_matrix(HD)), jnp.bfloat16)
     clip_start = (
         lax.dynamic_slice_in_dim(
@@ -972,33 +1199,19 @@
     w_in = small_low[FREQ + D : FREQ + D + P_SIZE]
     w_head = small_low[FREQ + D + P_SIZE :]
     inputs_low = inputs.astype(jnp.bfloat16)
-    shaped_zero = jnp.dot(inputs_low, w_in, preferred_element_type=jnp.float32).reshape(
-        frame_count, TPF, D
-    )
-    normed_one = (
-        modulate_local(shaped_zero, shift_one, scale_one).reshape(tok_count, D).astype(jnp.bfloat16)
-    )
-    turned_weights = jnp.einsum(
-        "kde,ef->kdf", w_attn[:2], rotation, preferred_element_type=jnp.bfloat16
-    )
-    projected = jnp.einsum(
-        "td,kde->kte", normed_one, w_attn[:3], preferred_element_type=jnp.float32
-    )
-    turned = jnp.einsum(
-        "td,kde->kte", normed_one, turned_weights, preferred_element_type=jnp.float32
-    )
-    queries = (projected[0] * cosine_table + turned[0] * sine_table).astype(jnp.bfloat16)
-    keys_own = (projected[1] * cosine_table + turned[1] * sine_table).astype(jnp.bfloat16)
-    values_own = projected[2].astype(jnp.bfloat16)
-    key_parts = [keys_own]
-    value_parts = [values_own]
-    for reach_step in range(1, REACH + 1):
-        far_keys, far_values = shifted((keys_own, values_own), "frames", reach_step)
-        key_parts.insert(0, far_keys)
-        value_parts.insert(0, far_values)
-    keys_wide = jnp.concatenate(key_parts, axis=0)
-    values_wide = jnp.concatenate(value_parts, axis=0)
-
+    padding = ((0, 0), (0, 128 - P_SIZE))
+    inputs_low = jnp.pad(inputs_low, padding)
+    normed_one, hidden_half, queries, keys_wide, values_wide = proj_block(
+        inputs_low,
+        jnp.pad(w_in, ((0, 128 - P_SIZE), (0, 0))),
+        jnp.stack([shift_one[:, 0], scale_one[:, 0]]),
+        w_attn[:3],
+        cosine_table,
+        sine_table,
+        turn_four,
+        REACH,
+        2,
+    )
     heads_wide, log_totals = attn_fwd(queries, keys_wide, values_wide, clip_start)
     half = tok_count // 2
     own_frames = frame_count // 2
@@ -1009,14 +1222,13 @@
 
     token_weight = jnp.repeat(noised, TPF) / (TPF * P_SIZE)
     grad_scale = 1.0 / jnp.maximum(noised_count, 1.0)
-    padding = ((0, 0), (0, 128 - P_SIZE))
     mod_mid = jnp.stack(
         [half_of(piece[:, 0]) for piece in (gate_one, shift_two, scale_two, gate_two)]
     )
-    d_mixed, d_shaped_one, d_mod_mid, loss_parts, grad_joint = mid_block(
+    d_mixed, d_shaped_one, d_mod_mid, loss_parts, grad_up, grad_rest = mid_block(
         heads_wide,
         w_attn[3],
-        half_of(shaped_zero.reshape(tok_count, D)),
+        hidden_half,
         mod_mid,
         jnp.pad(half_of(noise_patches), padding),
         jnp.broadcast_to(half_of(token_weight)[:, None], (half, 128)),
@@ -1028,26 +1240,28 @@
         0,
     )
     loss_own = jnp.sum(loss_parts)
-    sum_joint = lax.psum_scatter(grad_joint, "frames", scatter_dimension=0, tiled=True)
+    sum_up = lax.psum_scatter(grad_up, "frames", scatter_dimension=0, tiled=True)
+    sum_rest = lax.psum_scatter(grad_rest, "frames", scatter_dimension=0, tiled=True)
     d_queries, keys_grad_wide, values_grad_wide = attn_bwd(
         queries, keys_wide, values_wide, d_mixed, heads_wide, log_totals, clip_start
     )
-    d_queries, sum_joint = lax.optimization_barrier((d_queries, sum_joint))
+    d_queries, sum_up = lax.optimization_barrier((d_queries, sum_up))
     grad_qkv, grad_in, d_first_mods = tail_block(
         d_queries,
         normed_one,
         w_attn[:3],
-        cosine_table[:, : 4 * HD],
-        sine_table[:, : 4 * HD],
+        cosine_table,
+        sine_table,
         turn_four,
-        half_of(shaped_zero.reshape(tok_count, D)),
+        hidden_half,
         half_of(scale_one[:, 0]),
         d_shaped_one,
-        jnp.pad(half_of(inputs_low), padding),
+        half_of(inputs_low),
         keys_grad_wide,
         values_grad_wide,
         1,
     )
+    d_first_mods, sum_rest = lax.optimization_barrier((d_first_mods, sum_rest))
     grad_in = grad_in[:P_SIZE]
     flip = [(0, 1), (1, 0)]
     first_cols = jnp.concatenate([d_first_mods[0], d_first_mods[1], d_mod_mid[0]], axis=1)
@@ -1094,15 +1308,15 @@
         jnp.float32
     )
     ff_cols = mlp_weights.shape[2]
-    sum_joint = sum_joint.astype(jnp.float32)
-    sum_mlp = jnp.stack([sum_joint[:, :ff_cols], sum_joint[:, ff_cols : 2 * ff_cols]])
+    sum_rest = sum_rest.astype(jnp.float32)
+    sum_mlp = jnp.stack([sum_up.astype(jnp.float32), sum_rest[:, :ff_cols]])
     sum_attn = jnp.stack(
         [joined_sum[:, k * width_local : (k + 1) * width_local] for k in range(3)]
-        + [sum_joint[:, 2 * ff_cols : 2 * ff_cols + width_local]]
-    )
-    head_first = 2 * ff_cols + width_local
+        + [sum_rest[:, ff_cols : ff_cols + width_local]]
+    )
+    head_first = ff_cols + width_local
     ends = jnp.concatenate(
-        [joined_sum[:, 3 * width_local :], sum_joint[:, head_first : head_first + P_SIZE]], axis=1
+        [joined_sum[:, 3 * width_local :], sum_rest[:, head_first : head_first + P_SIZE]], axis=1
     ).T
     sum_ends = half_of(ends, 1) + lax.ppermute(
         lax.dynamic_slice_in_dim(ends, (1 - mp_index) * small_cols, small_cols, 1), "mp", flip

time: 1020 us -> 929 us (0.911)
  Pallas kernels: 267 us -> 388 us
  waiting for transfers between devices: 485 us -> 365 us
  starting transfers between devices: 52.6 us -> 6.05 us
  local copies, waits for them, and re-layouts: 71 us -> 45.9 us
  matrix products: 37.6 us -> 21.8 us
  other arithmetic: 42.6 us -> 30 us
    reduce_scatter x1 -> x2, waiting for transfers between devices: 217 us -> 108 us  [the longest x1 108 us: per_device(): lax.psum_scatter(grad_up, 'frames', scatter_dimension=0, tiled=True)]
    pallas_call x0 -> x1, Pallas kernels: none -> 94 us  [proj_block(): pl.pallas_call(proj_kernel, in_specs=[vm] * 7, out_specs=[vm] * 3 + [anym...]
    ppermute x8 -> x0, starting transfers between devices: 47 us -> none  [shifted(): return lax.ppermute(shard, axis, pairs)]
    ppermute x8 -> x0, waiting for transfers between devices: 46.5 us -> none  [shifted(): return lax.ppermute(shard, axis, pairs)]
    pallas_call x1, Pallas kernels: 76.6 us -> 109 us  [tail_block(): pl.pallas_call(tail_kernel, in_specs=[vm] * 10 + [anym] * 2, out_specs=[v...]
    dot_general x3 -> x0, matrix products: 18.1 us -> none  [the longest x1 7.93 us: per_device(): jnp.einsum('td,kde->kte', normed_one, turned_weights, preferred_element_t...]
    all_gather x1, waiting for transfers between devices: 41.9 us -> 57.1 us  [per_device(): w_mod = lax.all_gather(low_mod, 'frames', axis=0, tiled=True)]
  transfers between devices with their start and end apart: 20 -> 13, of which waited for: 11 -> 10; matrix products, arithmetic and copies ran while one was open for 11% -> 7% of each run, Pallas kernels for 6% -> 28%
where the time goes in v1:
time: 929 us; the launch traced here: 919 us
  Pallas kernels  388 us (42%)
  waiting for transfers between devices  365 us (39%)
  local copies, waits for them, and re-layouts  45.9 us (5%)
  blocking collectives  42.6 us (5%)
  other arithmetic  30 us (3%)
  matrix products  21.8 us (2%)
  between operations  19.6 us (2%)
    pallas_call x1, Pallas kernels, mid_block(): pl.pallas_call(functools.partial(mid_kernel, tp=tp), in_specs=[vm] * 7 +...  129 us
    pallas_call x1, Pallas kernels, tail_block(): pl.pallas_call(tail_kernel, in_specs=[vm] * 10 + [anym] * 2, out_specs=[v...  109 us
    reduce_scatter x1, waiting for transfers between devices, per_device(): lax.psum_scatter(grad_up, 'frames', scatter_dimension=0, tiled=True)  108 us
    pallas_call x1, Pallas kernels, proj_block(): pl.pallas_call(proj_kernel, in_specs=[vm] * 7, out_specs=[vm] * 3 + [anym...  94 us
    reduce_scatter x1, waiting for transfers between devices, per_device(): lax.psum_scatter(joined, 'frames', scatter_dimension=0, tiled=True)  70 us
    all_gather x1, waiting for transfers between devices, per_device(): w_mod = lax.all_gather(low_mod, 'frames', axis=0, tiled=True)  57.1 us
    all_gather x1, waiting for transfers between devices, per_device(): d_mod_all = lax.all_gather(d_mod_own, 'frames', axis=0, tiled=True)  46.1 us
    all_gather x1, waiting for transfers between devices, per_device(): lax.all_gather(attn_weights.astype(jnp.bfloat16), 'frames', axis=1, tiled...  42.3 us
  transfers between devices with their start and end apart: 13, of which 10 were waited for; matrix products, arithmetic and copies ran while one was open for 7% of the time, Pallas kernels for 28%

profile of v1, /device:TPU:0, one launch (start us, length us, event | category | flops | bytes accessed | tf_op | source)
XLA Modules:
  0.0 918.6 jit_solution(10173126154866175880)
XLA Ops:
  16.6 34.9 %all-reduce.5 = f32[256]{0:T(256)S(1)} all-reduce(f32[256]{0:T(256)S(1)} %dynamic-update-slice), channel_id=1, replica_groups=mesh['frames'=16,'mp'=2] {'frames'}, use_global_device_ids=true, to_apply=%add.5 | all-reduce | flops 256 | bytes 2048
  64.0 8.8 all-gather.7.cloned.1.call-done
  77.7 4.9 fusion.4
  82.6 42.3 %all-gather.11.cloned.1.call-done = bf16[4,1024,512]{2,1,0:T(8,128)(2,1)} async-done(((bf16[4,64,512]{2,1,0:T(8,128)(2,1)}), bf16[4,1024,512]{2,1,0:T(8,128)(2,1)}) %all-gather.11.cloned.1.call-update) | async-done | bytes 4194320 | tf_op jit(solution)/shard_map/all_gather | solution.py:1147
  124.9 2.3 slice_bitcast_fusion.2.wo_ref
  127.2 3.8 slice.166.w_ref
  131.0 57.1 %all-gather.9.cloned.1.call-done = bf16[1024,3072]{1,0:T(8,128)(2,1)} async-done(((bf16[64,3072]{1,0:T(8,128)(2,1)}), bf16[1024,3072]{1,0:T(8,128)(2,1)}) %all-gather.9.cloned.1.call-update) | async-done | bytes 6291472 | tf_op jit(solution)/shard_map/all_gather | solution.py:1150
  188.1 4.6 fusion.16
  192.7 7.7 all_gather.27
  201.8 94.0 %projection_forward.1 = (bf16[1024,1024]{1,0:T(8,128)(2,1)S(1)}, f32[512,1024]{1,0:T(8,128)}, bf16[1024,512]{1,0:T(8,128)(2,1)S(1)}, bf16[5120,512]{1,0:T(8,128)(2,1)}, bf16[5120,512]{1,0:T(8,128)(2,1)}) custom-call(bf16[1024,128]{1,0:T(8,128)(2,1)S(1)} %pad.16.inp_ref, bf16[128,1024]{1,0:T(8,128)(2,1)S(1)} %pad.17.win_ref, ...), custom_call_target="tpu_custom_call" | custom-call | flops 60000002048 | bytes 30000000 | tf_op jit(solution)/shard_map/projection_forward/pallas_call | solution.py:1090
  297.2 21.0 %attn_forward.1 = (f32[1024,512]{1,0:T(8,128)S(1)}, f32[4,8,1024]{2,1,0:T(8,128)S(1)}) custom-call(s32[2]{0:T(128)S(1)} %get-tuple-element.80.lo_ref, s32[2]{0:T(128)S(1)} %get-tuple-element.79.mid_ref, s32[2]{0:T(128)S(1)} %get-tuple-element.78.hi_ref, bf16[1024,512]{1,0:T(8,128)(2,1)S(1)} %get-tuple-element.41.q_ref, ...), custom_call_target="tpu_custom_call" | custom-call | flops 99999997952 | bytes 20000000 | tf_op jit(solution)/shard_map/attn_forward/pallas_call | solution.py:158
  321.2 6.2 slice_bitcast_fusion
  328.2 129.0 %feed_forward.1 = (bf16[1024,512]{1,0:T(8,128)(2,1)}, f32[512,1024]{1,0:T(8,128)}, f32[4,8,1024]{2,1,0:T(8,128)}, f32[64,128]{1,0:T(8,128)}, bf16[1024,2048]{1,0:T(8,128)(2,1)}, /*index=5*/bf16[1024,2688]{1,0:T(8,128)(2,1)}) custom-call(f32[1024,512]{1,0:T(8,128)} %copy-done.8, bf16[1024,512]{1,0:T(8,128)(2,1)} %slice_bitcast_fusion.2.wo_ref, ...), custom_call_target="tpu_custom_call" | custom-call | flops 40000000000 | bytes 30000000 | tf_op jit(solution)/shard_map/feed_forward/pallas_call | solution.py:546
  459.8 34.9 %attn_backward.1 = (f32[1024,512]{1,0:T(8,128)}, bf16[5120,512]{1,0:T(8,128)(2,1)}, bf16[5120,512]{1,0:T(8,128)(2,1)}) custom-call(s32[2]{0:T(128)} %copy-done.5, s32[2]{0:T(128)} %copy-done.4, s32[2]{0:T(128)} %copy-done.3, bf16[1024,512]{1,0:T(8,128)(2,1)} %copy-done.9, bf16[5120,512]{1,0:T(8,128)(2,1)} %get-tuple-element.42.k_ref, ...), custom_call_target="tpu_custom_call" | custom-call | flops 199999995904 | bytes 50000000 | tf_op jit(solution)/shard_map/attn_backward/pallas_call | solution.py:227
  494.7 107.7 %reduce-scatter.4.cloned.1.call-done = bf16[64,2048]{1,0:T(8,128)(2,1)} async-done(((bf16[1024,2048]{1,0:T(8,128)(2,1)}), bf16[64,2048]{1,0:T(8,128)(2,1)}) %reduce-scatter.4.cloned.1.call-update) | async-done | bytes 262160 | tf_op jit(solution)/shard_map/reduce_scatter | solution.py:1243
  602.4 109.1 %projection_backward.1 = (bf16[3,1024,512]{2,1,0:T(8,128)(2,1)}, f32[128,1024]{1,0:T(8,128)}, f32[2,8,1024]{2,1,0:T(8,128)}) custom-call(f32[1024,512]{1,0:T(8,128)} %get-tuple-element.50.dq_ref, bf16[1024,1024]{1,0:T(8,128)(2,1)} %copy-done.7, bf16[3,1024,512]{2,1,0:T(8,128)(2,1)} %slice.166.w_ref, f32[1024,256]{1,0:T(8,128)} %copy-done.1, ...), custom_call_target="tpu_custom_call" | custom-call | flops 20000000000 | bytes 30000000 | tf_op jit(solution)/shard_map/projection_backward/pallas_call | solution.py:849
  719.0 3.2 collective-permute-done
  735.9 70.0 %reduce-scatter.8.cloned.1.call-done = bf16[64,1552]{1,0:T(8,128)(2,1)} async-done(((bf16[1024,1552]{1,0:T(8,128)(2,1)}), bf16[64,1552]{1,0:T(8,128)(2,1)}) %reduce-scatter.8.cloned.1.call-update) | async-done | bytes 198672 | tf_op jit(solution)/shard_map/reduce_scatter | solution.py:1307
  806.7 46.1 %all-gather.15.cloned.1.call-done = f32[256,3072]{1,0:T(8,128)} async-done(((f32[16,3072]{1,0:T(8,128)}), f32[256,3072]{1,0:T(8,128)}) %all-gather.15.cloned.1.call-update) | async-done | bytes 3145744 | tf_op jit(solution)/shard_map/all_gather | solution.py:1280
  852.8 3.6 fusion.62
  862.7 2.3 fusion.57
  865.0 2.1 add_multiply_fusion.2
  867.9 4.1 fusion.55
  873.9 26.4 %all-gather.17.cloned.1.call-done = f32[264,1024]{0,1:T(8,128)} async-done(((f32[264,64]{0,1:T(8,128)}), f32[264,1024]{0,1:T(8,128)}) %all-gather.17.cloned.1.call-update) | async-done | bytes 1081360 | tf_op jit(solution)/shard_map/all_gather | solution.py:1287
  (236 shorter events, 72.8 us)
Async XLA Ops:
  7.2 47.8 %copy-start.40 = (f32[16,1024]{1,0:T(8,128)S(1)}, f32[16,1024]{1,0:T(8,128)}, u32[]{:S(2)}) copy-start(f32[16,1024]{1,0:T(8,128)} %param.18) | copy-start | bytes 196612
  7.3 65.6 %all-gather.7.cloned.1.call-start = ((), (), s32[]{:S(2)}) async-start(), calls=%async_computation.3 | async-start | bytes 2973696 | tf_op jit(solution)/shard_map/all_gather | solution.py:1151
  9.0 115.9 %all-gather.11.cloned.1.call-start = ((), (), s32[]{:S(2)}) async-start(), calls=%async_computation.5 | async-start | bytes 4456448 | tf_op jit(solution)/shard_map/all_gather | solution.py:1147
  10.8 177.3 %all-gather.9.cloned.1.call-start = ((), (), s32[]{:S(2)}) async-start(), calls=%async_computation.4 | async-start | bytes 6684672 | tf_op jit(solution)/shard_map/all_gather | solution.py:1150
  12.8 308.4 %all-gather.13.cloned.1.call-start = ((), (), s32[]{:S(2)}) async-start(), calls=%async_computation.6 | async-start | bytes 8912896 | tf_op jit(solution)/shard_map/all_gather | solution.py:1148
  13.7 43.4 %copy-start.41 = (f32[16,1024]{1,0:T(8,128)S(1)}, f32[16,1024]{1,0:T(8,128)}, u32[]{:S(2)}) copy-start(f32[16,1024]{1,0:T(8,128)} %param.19) | copy-start | bytes 196612
  13.8 588.6 %reduce-scatter.4.cloned.1.call-start = ((), (), s32[]{:S(2)}) async-start(), calls=%async_computation.7 | async-start | bytes 4456448 | tf_op jit(solution)/shard_map/reduce_scatter | solution.py:1243
  60.5 141.3 %copy-start = (f32[1024,256]{1,0:T(8,128)}, f32[1024,256]{1,0:T(8,128)S(1)}, u32[]{:S(2)}) copy-start(f32[1024,256]{1,0:T(8,128)S(1)} %copy.87.sin_ref) | copy-start | bytes 3145732
  61.0 140.8 %copy-start.1 = (f32[1024,256]{1,0:T(8,128)}, f32[1024,256]{1,0:T(8,128)S(1)}, u32[]{:S(2)}) copy-start(f32[1024,256]{1,0:T(8,128)S(1)} %copy.86.cos_ref) | copy-start | bytes 3145732
  61.0 236.2 %copy-start.3 = (s32[2]{0:T(128)}, s32[2]{0:T(128)S(1)}, u32[]{:S(2)}) copy-start(s32[2]{0:T(128)S(1)} %get-tuple-element.78.hi_ref) | copy-start | bytes 28
  61.0 236.2 %copy-start.4 = (s32[2]{0:T(128)}, s32[2]{0:T(128)S(1)}, u32[]{:S(2)}) copy-start(s32[2]{0:T(128)S(1)} %get-tuple-element.79.mid_ref) | copy-start | bytes 28
  61.0 236.2 %copy-start.5 = (s32[2]{0:T(128)}, s32[2]{0:T(128)S(1)}, u32[]{:S(2)}) copy-start(s32[2]{0:T(128)S(1)} %get-tuple-element.80.lo_ref) | copy-start | bytes 28
  297.2 21.0 %copy-start.2 = (s32[8,1024]{1,0:T(8,128)}, s32[8,1024]{1,0:T(8,128)S(1)}, u32[]{:S(2)}) copy-start(s32[8,1024]{1,0:T(8,128)S(1)} %broadcast_in_dim.26.cs_ref) | copy-start | bytes 98308
  457.3 260.1 %reduce-scatter.6.cloned.1.call-start = ((), (), s32[]{:S(2)}) async-start(), calls=%async_computation.8 | async-start | bytes 5849088 | tf_op jit(solution)/shard_map/reduce_scatter | solution.py:1244
  459.5 346.4 %reduce-scatter.8.cloned.1.call-start = ((), (), s32[]{:S(2)}) async-start(), calls=%async_computation.11 | async-start | bytes 3620864 | tf_op jit(solution)/shard_map/reduce_scatter | solution.py:1307
  716.5 136.3 %all-gather.15.cloned.1.call-start = ((), (), s32[]{:S(2)}) async-start(), calls=%async_computation.9 | async-start | bytes 3342336 | tf_op jit(solution)/shard_map/all_gather | solution.py:1280
  717.5 4.8 collective-permute-start
  723.0 177.3 %all-gather.17.cloned.1.call-start = ((), (), s32[]{:S(2)}) async-start(), calls=%async_computation.10 | async-start | bytes 1671168 | tf_op jit(solution)/shard_map/all_gather | solution.py:1287
  725.6 3.6 collective-permute-start.2
  732.4 120.4 %copy-start.15 = (bf16[64,3072]{1,0:T(8,128)(2,1)S(1)}, bf16[64,3072]{1,0:T(8,128)(2,1)}, u32[]{:S(2)}) copy-start(bf16[64,3072]{1,0:T(8,128)(2,1)} %convert_element_type.83) | copy-start | bytes 1179652
  805.9 53.3 %copy-start.34 = (bf16[64,1552]{1,0:T(8,128)(2,1)S(1)}, bf16[64,1552]{1,0:T(8,128)(2,1)}, u32[]{:S(2)}) copy-start(bf16[64,1552]{1,0:T(8,128)(2,1)} %reduce-scatter.8.cloned.1.call-done) | copy-start | bytes 595972
  856.4 4.3 collective-permute-start.1
  858.7 8.4 collective-permute-start.3
  873.8 29.7 %copy-start.23 = (f32[256,1024]{1,0:T(8,128)S(1)}, f32[256,1024]{1,0:T(8,128)}, u32[]{:S(2)}) copy-start(f32[256,1024]{1,0:T(8,128)} %copy-done.22) | copy-start | bytes 3145732
  (39 other events, 233.2 us)
Sparse Core Ops, SparseCore 0:
  11.5 61.3 all-gather.6
  75.6 49.2 all-gather.10
  127.8 60.3 all-gather.8
  190.7 102.2 all-gather.12
  457.4 144.9 reduce-scatter.3
  606.6 104.1 reduce-scatter.5
  716.6 89.1 reduce-scatter.7
  808.7 44.0 all-gather.14
  861.6 38.6 all-gather.16

commit v2 on v1

--- a/solution.py
+++ b/solution.py
@@ -618,6 +618,7 @@
     f32, bf16 = jnp.float32, jnp.bfloat16
     MESH = pl.DeviceIdType.MESH
     sides = (dk_hbm, dv_hbm)
+    share = width // n
 
     def at(start, size):
         return pl.ds(pl.multiple_of(start, size), size)
@@ -744,8 +745,12 @@
 
     def grads(k):
         def tile(i, _):
-            d = at(i * 256, 256)
-            gq_ref[k, d, :] = dotf(n1t[d, :], dproj[k]).astype(bf16)
+            res = dotf(n1t[at(i * 256, 256), :], dproj[k]).astype(bf16)
+            for q in range(256 // share):
+                j = i * (256 // share // 4) + q // 4
+                gq_ref[q % 2, (q // 2) % 2, k, at(j * share, share), :] = res[
+                    q * share : (q + 1) * share
+                ]
             return 0
 
         lax.fori_loop(0, width // 256, tile, 0)
@@ -851,7 +856,7 @@
         in_specs=[vm] * 10 + [anym] * 2,
         out_specs=[vm] * 3,
         out_shape=[
-            jax.ShapeDtypeStruct((3, width, e), bf16),
+            jax.ShapeDtypeStruct((2, 2, 3, width // 4, e), bf16),
             jax.ShapeDtypeStruct((128, width), f32),
             jax.ShapeDtypeStruct((2, half // TPF, width), f32),
         ],
@@ -1111,6 +1116,251 @@
         ),
         name="projection_forward",
     )(inp, win, mod, w, cosine, sine, rot)
+
+
+def last_kernel(
+    g_hbm, gin_ref, dm_ref, cond_ref, wm_ref, loss_ref,
+    sq_ref, sin_ref, smod_ref, dct_ref,
+    g_own, g_in, near, near_in, side, side_in, far, far_in, ends, ends_peer, dm_peer, dm,
+    dc_send, dc_peer,
+    lsem, s_x, r_x, s_g, r_g, s_f, r_f, s_d, r_d, s_dz, r_dz,
+):
+    f = lax.axis_index("frames")
+    h = lax.axis_index("mp")
+    n = lax.axis_size("frames")
+    nj = n // 4
+    core = lax.rem(f, 2)
+    y = lax.rem(lax.div(f, 2), 2)
+    j = lax.div(f, 4)
+    core_peer = {"frames": f + 1 - 2 * core}
+    y_peer = {"frames": f + 2 - 4 * y}
+    x_peer = {"mp": 1 - h}
+    f32, bf16 = jnp.float32, jnp.bfloat16
+    MESH = pl.DeviceIdType.MESH
+    rows = g_hbm.shape[3] // nj
+
+    def z_peer(t):
+        return {"frames": lax.rem(f + 4 * t, n)}
+
+    def from_j(t):
+        return lax.rem(j - t + nj, nj)
+
+    def at(start, size):
+        return pl.ds(pl.multiple_of(start, size), size)
+
+    load = pltpu.make_async_copy(g_hbm.at[core], g_own, lsem.at[0])
+    load.start()
+    barrier = pltpu.get_barrier_semaphore()
+    for peer in [core_peer, y_peer, x_peer] + [z_peer(t) for t in range(1, nj)]:
+        pl.semaphore_signal(barrier, inc=1, device_id=peer, device_id_type=MESH)
+    pl.semaphore_wait(barrier, 2 + nj)
+
+    def remote(src, dst, send, recv, peer):
+        return pltpu.make_async_remote_copy(
+            src_ref=src, dst_ref=dst, send_sem=send, recv_sem=recv, device_id=peer,
+            device_id_type=MESH,
+        )
+
+    dm_x = remote(dm_ref.at[1 - h], dm_peer, s_x.at[0], r_x.at[0], x_peer)
+    dm_x.start()
+    core_g = remote(g_hbm.at[1 - core], near, s_g.at[0], r_g.at[0], core_peer)
+    core_in = remote(gin_ref.at[1 - core], near_in, s_g.at[1], r_g.at[1], core_peer)
+    core_g.start()
+    core_in.start()
+
+    dm_x.wait_recv()
+    mine = dm_ref[h]
+    theirs = dm_peer[...]
+    low = h == 0
+    dm[core, y, j] = jnp.concatenate(
+        [jnp.where(low, mine, theirs), jnp.where(low, theirs, mine)], axis=0
+    ).astype(bf16)
+
+    def dm_z(t, src):
+        block = dm.at[core, y, src]
+        return remote(block, block, s_dz.at[0, t], r_dz.at[0, t], z_peer(t))
+
+    for t in range(1, nj):
+        dm_z(t, j).start()
+    load.wait()
+    core_g.wait_recv()
+    core_in.wait_recv()
+
+    def add_near(i, _):
+        for s in range(2):
+            for k in range(g_own.shape[1]):
+                r = at(i * rows, rows)
+                g_own[s, k, r, :] = (
+                    g_own[s, k, r, :].astype(f32) + near[s, k, r, :].astype(f32)
+                ).astype(bf16)
+        return 0
+
+    lax.fori_loop(0, nj, add_near, 0)
+    g_in[...] = (gin_ref[core].astype(f32) + near_in[...].astype(f32)).astype(bf16)
+    for t in range(1, nj):
+        dm_z(t, from_j(t)).wait_recv()
+
+    def dm_y(side_index):
+        block = dm.at[core, side_index]
+        return remote(block, block, s_d.at[0], r_d.at[0], y_peer)
+
+    dm_y(y).start()
+    y_g = remote(g_own.at[1 - y], side, s_g.at[2], r_g.at[2], y_peer)
+    y_in = remote(g_in.at[1 - y], side_in, s_g.at[3], r_g.at[3], y_peer)
+    y_g.start()
+    y_in.start()
+    dm_y(1 - y).wait_recv()
+
+    def dm_core(core_index):
+        block = dm.at[core_index]
+        return remote(block, block, s_d.at[1], r_d.at[1], core_peer)
+
+    dm_core(core).start()
+    y_g.wait_recv()
+    y_in.wait_recv()
+
+    def add_side(i, _):
+        for k in range(g_own.shape[1]):
+            r = at(i * rows, rows)
+            side[k, r, :] = (
+                g_own[y, k, r, :].astype(f32) + side[k, r, :].astype(f32)
+            ).astype(bf16)
+        return 0
+
+    lax.fori_loop(0, nj, add_side, 0)
+    side_in[...] = (g_in[y].astype(f32) + side_in[...].astype(f32)).astype(bf16)
+
+    def far_g(t):
+        there = at(lax.rem(j + t, nj) * rows, rows)
+        return remote(
+            side.at[:, there], far.at[t - 1], s_f.at[0, t], r_f.at[0, t], z_peer(t)
+        )
+
+    def far_i(t):
+        there = at(lax.rem(j + t, nj) * rows, rows)
+        return remote(
+            side_in.at[there], far_in.at[t - 1], s_f.at[1, t], r_f.at[1, t], z_peer(t)
+        )
+
+    for t in range(1, nj):
+        far_g(t).start()
+        far_i(t).start()
+
+    dm_core(1 - core).wait_recv()
+    frames = dm.shape[0] * dm.shape[1] * dm.shape[2] * dm.shape[3]
+    wide = dm.shape[4]
+    every = dm[...].reshape(frames, wide)
+    part = dotf(wm_ref[...], every, NT)
+    dc_send[:rows, :] = part
+    dc_send[rows:, :] = jnp.broadcast_to(jnp.sum(loss_ref[...]), (8, frames))
+    dc_x = remote(dc_send, dc_peer, s_x.at[1], r_x.at[1], x_peer)
+    dc_x.start()
+
+    def mod_cols(i, _):
+        cols = at(i * 512, 512)
+        block = dm[:, :, :, :, cols].reshape(frames, 512)
+        res = dotf(cond_ref[...], block)
+        smod_ref[:, cols] = res[:rows] + res[rows : 2 * rows] + res[2 * rows :]
+        return 0
+
+    lax.fori_loop(0, wide // 512, mod_cols, 0)
+    dc_x.wait_recv()
+    total = dc_send[...] + dc_peer[...]
+    dct_ref[core, y, j, :rows, :] = total[:rows].astype(bf16)
+    pieces = [p[:1].astype(f32) for p in split_three(total[rows:])]
+    dct_ref[core, y, j, rows:, :] = jnp.concatenate(
+        pieces + [jnp.zeros((13, frames), f32)], axis=0
+    ).astype(bf16)
+
+    def dc_z(t, src):
+        block = dct_ref.at[core, y, src]
+        return remote(block, block, s_dz.at[1, t], r_dz.at[1, t], z_peer(t))
+
+    for t in range(1, nj):
+        dc_z(t, j).start()
+    for t in range(1, nj):
+        dc_z(t, from_j(t)).wait_recv()
+
+    def dc_y(side_index):
+        block = dct_ref.at[core, side_index]
+        return remote(block, block, s_d.at[2], r_d.at[2], y_peer)
+
+    dc_y(y).start()
+
+    here = at(j * rows, rows)
+    for t in range(1, nj):
+        far_g(t).wait_recv()
+        far_i(t).wait_recv()
+    for k in range(sq_ref.shape[0]):
+        sq_ref[k] = side[k, here, :].astype(f32) + sum(
+            far[t, k].astype(f32) for t in range(nj - 1)
+        )
+    ends[...] = side_in[here, :].astype(f32) + sum(
+        far_in[t].astype(f32) for t in range(nj - 1)
+    )
+    ends_x = remote(ends, ends_peer, s_x.at[2], r_x.at[2], x_peer)
+    ends_x.start()
+    dc_y(1 - y).wait_recv()
+
+    def dc_core(core_index):
+        block = dct_ref.at[core_index]
+        return remote(block, block, s_d.at[3], r_d.at[3], core_peer)
+
+    dc_core(core).start()
+    ends_x.wait_recv()
+    sin_ref[...] = ends[...] + ends_peer[...]
+    dc_core(1 - core).wait_recv()
+
+    for one in (dm_x, core_g, core_in, y_g, y_in, dc_x, ends_x):
+        one.wait_send()
+    for one in (dm_y(y), dm_core(core), dc_y(y), dc_core(core)):
+        one.wait_send()
+    for t in range(1, nj):
+        for one in (dm_z(t, j), dc_z(t, j), far_g(t), far_i(t)):
+            one.wait_send()
+
+
+def last_block(g, gin, dm, cond, wm, loss, cid):
+    _, _, kinds, block_rows, e = g.shape
+    n = lax.axis_size("frames")
+    nj = n // 4
+    rows = block_rows // nj
+    own_frames, wide = dm.shape[1:]
+    frames = n * 2 * own_frames
+    f32, bf16 = jnp.float32, jnp.bfloat16
+    vm = pl.BlockSpec(memory_space=pltpu.VMEM)
+    anym = pl.BlockSpec(memory_space=pl.ANY)
+    V = pltpu.VMEM
+    D_ = pltpu.SemaphoreType.DMA
+    return pl.pallas_call(
+        last_kernel,
+        in_specs=[anym] + [vm] * 5,
+        out_specs=[vm] * 4,
+        out_shape=[
+            jax.ShapeDtypeStruct((kinds, rows, e), f32),
+            jax.ShapeDtypeStruct((rows, 128), f32),
+            jax.ShapeDtypeStruct((rows, wide), f32),
+            jax.ShapeDtypeStruct((2, 2, nj, rows + 16, frames), bf16),
+        ],
+        scratch_shapes=[
+            V((2, kinds, block_rows, e), bf16), V((2, block_rows, 128), bf16),
+            V((2, kinds, block_rows, e), bf16), V((2, block_rows, 128), bf16),
+            V((kinds, block_rows, e), bf16), V((block_rows, 128), bf16),
+            V((nj - 1, kinds, rows, e), bf16), V((nj - 1, rows, 128), bf16),
+            V((rows, 128), f32), V((rows, 128), f32),
+            V((own_frames, wide), f32), V((2, 2, nj, 2 * own_frames, wide), bf16),
+            V((rows + 8, frames), f32), V((rows + 8, frames), f32),
+            D_((1,)), D_((3,)), D_((3,)), D_((4,)), D_((4,)), D_((2, nj)), D_((2, nj)),
+            D_((4,)), D_((4,)), D_((2, nj)), D_((2, nj)),
+        ],
+        compiler_params=pltpu.CompilerParams(
+            vmem_limit_bytes=48 << 20, collective_id=cid, has_side_effects=True
+        ),
+        cost_estimate=pl.CostEstimate(
+            flops=2 * 10**10, bytes_accessed=2 * 10**7, transcendentals=0
+        ),
+        name="weight_sums",
+    )(g, gin, dm, cond, wm, loss)
 
 
 def per_device(
@@ -1187,6 +1437,25 @@
     first_all = jax.nn.silu(pre_one)
     pre_two = jnp.dot(first_all, small_full[FREQ : FREQ + D], precision=HIGH)
     conditioning_all = jax.nn.silu(pre_two)
+    placed = jnp.asarray(
+        np.arange(frames_total)
+        .reshape(-1, 2, 2, frame_count)
+        .transpose(2, 1, 0, 3)
+        .reshape(frames_total)
+    )
+    features_placed = features_all[placed]
+    first_placed = first_all[placed]
+    pre_two_t = pre_two[placed].T
+    pre_one_own = lax.dynamic_slice_in_dim(
+        pre_one,
+        (device * lax.axis_size("mp") + mp_index) * small_weights.shape[1],
+        small_weights.shape[1],
+        1,
+    )[placed].T
+    cond_rows = lax.dynamic_slice_in_dim(
+        conditioning_all, device * mod_weight.shape[0], mod_weight.shape[0], 1
+    )[placed]
+    cond_parts = jnp.concatenate([part.T for part in split_three(cond_rows)], axis=0)
     conditioning = lax.dynamic_slice_in_dim(conditioning_all, first_frame, frame_count)
     mod_full = w_mod.astype(jnp.float32)
     modulation = lax.all_gather(
@@ -1239,7 +1508,6 @@
         TP_AXIS,
         0,
     )
-    loss_own = jnp.sum(loss_parts)
     sum_up = lax.psum_scatter(grad_up, "frames", scatter_dimension=0, tiled=True)
     sum_rest = lax.psum_scatter(grad_rest, "frames", scatter_dimension=0, tiled=True)
     d_queries, keys_grad_wide, values_grad_wide = attn_bwd(
@@ -1262,65 +1530,51 @@
         1,
     )
     d_first_mods, sum_rest = lax.optimization_barrier((d_first_mods, sum_rest))
-    grad_in = grad_in[:P_SIZE]
-    flip = [(0, 1), (1, 0)]
-    first_cols = jnp.concatenate([d_first_mods[0], d_first_mods[1], d_mod_mid[0]], axis=1)
-    later_cols = jnp.concatenate([d_mod_mid[1], d_mod_mid[2], d_mod_mid[3]], axis=1)
-    kept_cols = jnp.where(mp_index == 0, first_cols, later_cols)
-    their_cols = lax.ppermute(jnp.where(mp_index == 0, later_cols, first_cols), "mp", flip)
-    d_mod_own = jnp.concatenate(
-        [
-            jnp.where(mp_index == 0, kept_cols, their_cols),
-            jnp.where(mp_index == 0, their_cols, kept_cols),
-        ],
-        axis=0,
-    )
+    frame_groups = frames_total // (4 * frame_count)
     mod_rows = mod_weight.shape[0]
     small_cols = small_weights.shape[1]
-    d_mod_all = lax.all_gather(d_mod_own, "frames", axis=0, tiled=True)
-    cond_rows = lax.dynamic_slice_in_dim(conditioning_all, device * mod_rows, mod_rows, 1)
-    sum_mod = jnp.einsum("fr,fc->rc", cond_rows, d_mod_all, precision=HIGH)
-    d_cond_part = jnp.einsum("fc,rc->fr", d_mod_all, low_mod.astype(jnp.float32), precision=HIGH)
-    loss_both = loss_own + lax.ppermute(loss_own, "mp", flip)
-    loss_rows = jnp.broadcast_to(loss_both, (8, mod_rows))
-    d_cond_rows = jnp.concatenate([d_cond_part + lax.ppermute(d_cond_part, "mp", flip), loss_rows], axis=0)
-    d_cond_all = lax.all_gather(d_cond_rows, "frames", axis=1, tiled=True)
-    loss_sum = jnp.sum(d_cond_all[frames_total]) / mod_rows
-    d_pre_two = jax.vjp(jax.nn.silu, pre_two)[1](d_cond_all[:frames_total])[0]
+
+    def by_place(array, dim):
+        shape = array.shape
+        size = shape[dim] // (4 * frame_groups)
+        split = array.reshape(shape[:dim] + (frame_groups, 2, 2, size) + shape[dim + 1 :])
+        order = list(range(split.ndim))
+        order[dim], order[dim + 2] = dim + 2, dim
+        return split.transpose(order)
+
+    in_columns = by_place(grad_in.T, 0).reshape(2, 2, D // 4, 128).astype(jnp.bfloat16)
+    d_mods = jnp.stack(
+        [
+            jnp.concatenate([d_first_mods[0], d_first_mods[1], d_mod_mid[0]], axis=1),
+            jnp.concatenate([d_mod_mid[1], d_mod_mid[2], d_mod_mid[3]], axis=1),
+        ]
+    )
+    sum_qkv, sum_in, sum_mod, d_cond_rows = last_block(
+        grad_qkv, in_columns, d_mods, cond_parts, low_mod, loss_parts, 3
+    )
+    loss_sum = jnp.sum(d_cond_rows[:, :, :, mod_rows : mod_rows + 3, 0].astype(jnp.float32))
+    d_cond_t = (
+        d_cond_rows[:, :, :, :mod_rows, :].transpose(2, 1, 0, 3, 4).reshape(D, frames_total)
+    ).astype(jnp.float32)
+    d_pre_two = jax.vjp(jax.nn.silu, pre_two_t)[1](d_cond_t)[0]
     first_col = (device * lax.axis_size("mp") + mp_index) * small_cols
-
-    def own(array):
-        return lax.dynamic_slice_in_dim(array, first_col, small_cols, 1)
-
-    grad_second = jnp.einsum("fi,fj->ij", first_all, own(d_pre_two), precision=HIGH)
+    d_pre_own = lax.dynamic_slice_in_dim(d_pre_two, first_col, small_cols, 0)
+    grad_second = jnp.einsum("fi,jf->ij", first_placed, d_pre_own, precision=HIGH)
     second_rows = lax.dynamic_slice_in_dim(small_full, FREQ + first_col, small_cols, 0)
-    d_first = jnp.einsum("fk,jk->fj", d_pre_two, second_rows, precision=HIGH)
-    d_pre_one = jax.vjp(jax.nn.silu, own(pre_one))[1](d_first)[0]
-    grad_first = jnp.einsum("fi,fj->ij", features_all, d_pre_one, precision=HIGH)
-    joined = jnp.concatenate(
-        [
-            part.astype(jnp.bfloat16)
-            for part in (grad_qkv[0], grad_qkv[1], grad_qkv[2], grad_in.T)
-        ],
-        axis=1,
-    )
-    joined_sum = lax.psum_scatter(joined, "frames", scatter_dimension=0, tiled=True).astype(
-        jnp.float32
-    )
+    d_first = jnp.einsum("kf,jk->jf", d_pre_two, second_rows, precision=HIGH)
+    d_pre_one = jax.vjp(jax.nn.silu, pre_one_own)[1](d_first)[0]
+    grad_first = jnp.einsum("fi,jf->ij", features_placed, d_pre_one, precision=HIGH)
     ff_cols = mlp_weights.shape[2]
     sum_rest = sum_rest.astype(jnp.float32)
     sum_mlp = jnp.stack([sum_up.astype(jnp.float32), sum_rest[:, :ff_cols]])
     sum_attn = jnp.stack(
-        [joined_sum[:, k * width_local : (k + 1) * width_local] for k in range(3)]
+        [sum_qkv[0], sum_qkv[1], sum_qkv[2]]
         + [sum_rest[:, ff_cols : ff_cols + width_local]]
     )
     head_first = ff_cols + width_local
-    ends = jnp.concatenate(
-        [joined_sum[:, 3 * width_local :], sum_rest[:, head_first : head_first + P_SIZE]], axis=1
-    ).T
-    sum_ends = half_of(ends, 1) + lax.ppermute(
-        lax.dynamic_slice_in_dim(ends, (1 - mp_index) * small_cols, small_cols, 1), "mp", flip
-    )
+    head_part = sum_rest[:, head_first : head_first + P_SIZE]
+    sum_head = head_part + lax.ppermute(head_part, "mp", [(0, 1), (1, 0)])
+    sum_ends = half_of(jnp.concatenate([sum_in[:, :P_SIZE], sum_head], axis=1).T, 1)
     sum_small = jnp.concatenate([grad_first, grad_second, sum_ends], axis=0)
     learning_rate = 0.5 * math.sqrt(tokens_total * P_SIZE / D)
     attn_new, attn_moment_new, attn_average_new, attn_copy = update(

time: 929 us -> 845 us (0.910)
  waiting for transfers between devices: 365 us -> 194 us
  Pallas kernels: 388 us -> 480 us
    pallas_call x0 -> x1, Pallas kernels: none -> 75 us  [last_block(): pl.pallas_call(last_kernel, in_specs=[anym] + [vm] * 5, out_specs=[vm] *...]
    all_gather x2 -> x0, waiting for transfers between devices: 72.6 us -> none  [the longest x1 46.1 us: per_device(): d_mod_all = lax.all_gather(d_mod_own, 'frames', axis=0, tiled=True)]
    reduce_scatter x1 -> x0, waiting for transfers between devices: 70 us -> none  [per_device(): lax.psum_scatter(joined, 'frames', scatter_dimension=0, tiled=True)]
    reduce_scatter x1, waiting for transfers between devices: 108 us -> 87 us  [per_device(): lax.psum_scatter(grad_up, 'frames', scatter_dimension=0, tiled=True)]
    pallas_call x1, Pallas kernels: 109 us -> 126 us  [tail_block(): pl.pallas_call(tail_kernel, in_specs=[vm] * 10 + [anym] * 2, out_specs=[v...]
  transfers between devices with their start and end apart: 13 -> 7, of which waited for: 10 -> 4; matrix products, arithmetic and copies ran while one was open for 7% -> 9% of each run, Pallas kernels for 28% -> 42%
where the time goes in v2:
time: 845 us; the launch traced here: 828 us
  Pallas kernels  480 us (57%)
  waiting for transfers between devices  194 us (23%)
  local copies, waits for them, and re-layouts  50.5 us (6%)
  blocking collectives  42.8 us (5%)
  other arithmetic  28 us (3%)
  between operations  16.8 us (2%)
  matrix products  13.6 us (2%)
    pallas_call x1, Pallas kernels, mid_block(): pl.pallas_call(functools.partial(mid_kernel, tp=tp), in_specs=[vm] * 7 +...  129 us
    pallas_call x1, Pallas kernels, tail_block(): pl.pallas_call(tail_kernel, in_specs=[vm] * 10 + [anym] * 2, out_specs=[v...  126 us
    pallas_call x1, Pallas kernels, proj_block(): pl.pallas_call(proj_kernel, in_specs=[vm] * 7, out_specs=[vm] * 3 + [anym...  94 us
    reduce_scatter x1, waiting for transfers between devices, per_device(): lax.psum_scatter(grad_up, 'frames', scatter_dimension=0, tiled=True)  87 us
    pallas_call x1, Pallas kernels, last_block(): pl.pallas_call(last_kernel, in_specs=[anym] + [vm] * 5, out_specs=[vm] *...  75 us
    all_gather x1, waiting for transfers between devices, per_device(): w_mod = lax.all_gather(low_mod, 'frames', axis=0, tiled=True)  57.1 us
    all_gather x1, waiting for transfers between devices, per_device(): lax.all_gather(attn_weights.astype(jnp.bfloat16), 'frames', axis=1, tiled...  42.5 us
    pallas_call x1, Pallas kernels, attn_bwd(): pl.pallas_call(functools.partial(bwd_kernel, TQ=TQ, TK=TK, W0=W0, NQ=NQ),...  35 us
  transfers between devices with their start and end apart: 7, of which 4 were waited for; matrix products, arithmetic and copies ran while one was open for 9% of the time, Pallas kernels for 42%

profile of v2, /device:TPU:0, one launch (start us, length us, event | category | flops | bytes accessed | tf_op | source)
XLA Modules:
  0.0 828.2 jit_solution(10621072454289695312)
XLA Ops:
  12.8 2.1 convert_element_type.129
  17.8 35.0 %all-reduce.4 = f32[256]{0:T(256)S(1)} all-reduce(f32[256]{0:T(256)S(1)} %dynamic-update-slice), channel_id=1, replica_groups=mesh['frames'=16,'mp'=2] {'frames'}, use_global_device_ids=true, to_apply=%add.4 | all-reduce | flops 256 | bytes 2048
  65.3 7.5 all-gather.5.cloned.1.call-done
  75.0 3.0 divide_multiply_fusion.1
  79.0 3.3 divide_multiply_fusion
  82.3 42.5 %all-gather.9.cloned.1.call-done = bf16[4,1024,512]{2,1,0:T(8,128)(2,1)} async-done(((bf16[4,64,512]{2,1,0:T(8,128)(2,1)}), bf16[4,1024,512]{2,1,0:T(8,128)(2,1)}) %all-gather.9.cloned.1.call-update) | async-done | bytes 4194320 | tf_op jit(solution)/shard_map/all_gather | solution.py:1397
  124.8 2.3 slice_bitcast_fusion.2.wo_ref
  127.1 3.8 slice.151.w_ref
  131.0 57.1 %all-gather.7.cloned.1.call-done = bf16[1024,3072]{1,0:T(8,128)(2,1)} async-done(((bf16[64,3072]{1,0:T(8,128)(2,1)}), bf16[1024,3072]{1,0:T(8,128)(2,1)}) %all-gather.7.cloned.1.call-update) | async-done | bytes 6291472 | tf_op jit(solution)/shard_map/all_gather | solution.py:1400
  188.1 4.6 fusion.13
  192.7 7.7 all_gather.21
  201.8 94.0 %projection_forward.1 = (bf16[1024,1024]{1,0:T(8,128)(2,1)S(1)}, f32[512,1024]{1,0:T(8,128)}, bf16[1024,512]{1,0:T(8,128)(2,1)S(1)}, bf16[5120,512]{1,0:T(8,128)(2,1)}, bf16[5120,512]{1,0:T(8,128)(2,1)}) custom-call(bf16[1024,128]{1,0:T(8,128)(2,1)S(1)} %pad.15.inp_ref, bf16[128,1024]{1,0:T(8,128)(2,1)S(1)} %pad.16.win_ref, ...), custom_call_target="tpu_custom_call" | custom-call | flops 60000002048 | bytes 30000000 | tf_op jit(solution)/shard_map/projection_forward/pallas_call | solution.py:1095
  297.2 21.0 %attn_forward.1 = (f32[1024,512]{1,0:T(8,128)S(1)}, f32[4,8,1024]{2,1,0:T(8,128)S(1)}) custom-call(s32[2]{0:T(128)S(1)} %get-tuple-element.88.lo_ref, s32[2]{0:T(128)S(1)} %get-tuple-element.87.mid_ref, s32[2]{0:T(128)S(1)} %get-tuple-element.86.hi_ref, bf16[1024,512]{1,0:T(8,128)(2,1)S(1)} %get-tuple-element.45.q_ref, ...), custom_call_target="tpu_custom_call" | custom-call | flops 99999997952 | bytes 20000000 | tf_op jit(solution)/shard_map/attn_forward/pallas_call | solution.py:158
  321.2 6.2 slice_bitcast_fusion
  328.2 129.0 %feed_forward.1 = (bf16[1024,512]{1,0:T(8,128)(2,1)}, f32[512,1024]{1,0:T(8,128)}, f32[4,8,1024]{2,1,0:T(8,128)}, f32[64,128]{1,0:T(8,128)}, bf16[1024,2048]{1,0:T(8,128)(2,1)}, /*index=5*/bf16[1024,2688]{1,0:T(8,128)(2,1)}) custom-call(f32[1024,512]{1,0:T(8,128)} %copy-done.10, bf16[1024,512]{1,0:T(8,128)(2,1)} %slice_bitcast_fusion.2.wo_ref, ...), custom_call_target="tpu_custom_call" | custom-call | flops 40000000000 | bytes 30000000 | tf_op jit(solution)/shard_map/feed_forward/pallas_call | solution.py:546
  460.6 2.0 gather_fusion.4
  465.1 2.0 gather_fusion.2
  469.7 35.0 %attn_backward.1 = (f32[1024,512]{1,0:T(8,128)}, bf16[5120,512]{1,0:T(8,128)(2,1)}, bf16[5120,512]{1,0:T(8,128)(2,1)}) custom-call(s32[2]{0:T(128)} %copy-done.6, s32[2]{0:T(128)} %copy-done.5, s32[2]{0:T(128)} %copy-done.4, bf16[1024,512]{1,0:T(8,128)(2,1)} %copy-done.11, bf16[5120,512]{1,0:T(8,128)(2,1)} %get-tuple-element.46.k_ref, ...), custom_call_target="tpu_custom_call" | custom-call | flops 199999995904 | bytes 50000000 | tf_op jit(solution)/shard_map/attn_backward/pallas_call | solution.py:227
  504.8 87.0 %reduce-scatter.3.cloned.1.call-done = bf16[64,2048]{1,0:T(8,128)(2,1)} async-done(((bf16[1024,2048]{1,0:T(8,128)(2,1)}), bf16[64,2048]{1,0:T(8,128)(2,1)}) %reduce-scatter.3.cloned.1.call-update) | async-done | bytes 262160 | tf_op jit(solution)/shard_map/reduce_scatter | solution.py:1511
  591.8 126.1 %projection_backward.1 = (bf16[2,2,3,256,512]{4,3,2,1,0:T(8,128)(2,1)}, f32[128,1024]{1,0:T(8,128)}, f32[2,8,1024]{2,1,0:T(8,128)}) custom-call(f32[1024,512]{1,0:T(8,128)} %get-tuple-element.54.dq_ref, bf16[1024,1024]{1,0:T(8,128)(2,1)} %copy-done.9, bf16[3,1024,512]{2,1,0:T(8,128)(2,1)} %slice.151.w_ref, f32[1024,256]{1,0:T(8,128)} %copy-done.2, ...), custom_call_target="tpu_custom_call" | custom-call | flops 20000000000 | bytes 30000000 | tf_op jit(solution)/shard_map/projection_backward/pallas_call | solution.py:854
  726.1 75.0 %weight_sums.1 = (f32[3,64,512]{2,1,0:T(8,128)S(1)}, f32[64,128]{1,0:T(8,128)S(1)}, f32[64,3072]{1,0:T(8,128)S(1)}, bf16[2,2,4,80,256]{4,3,2,1,0:T(8,128)(2,1)S(1)}) custom-call(bf16[2,2,3,256,512]{4,3,2,1,0:T(8,128)(2,1)S(1)} %copy-done.8, bf16[2,2,256,128]{3,2,1,0:T(8,128)(2,1)S(1)} %bitcast.123, f32[2,8,3072]{2,1,0:T(8,128)S(1)} %pad_maximum_fusion.3.dm_ref, ...), custom_call_target="tpu_custom_call" | custom-call | flops 20000000000 | bytes 20000000 | tf_op jit(solution)/shard_map/weight_sums/pallas_call | solution.py:1335
  802.3 2.5 copy.100
  804.8 2.4 fusion.46
  807.3 2.1 add_multiply_fusion.2
  (239 shorter events, 57.8 us)
Async XLA Ops:
  7.2 9.1 %copy-start.55 = (u32[32]{0:T(128)S(1)}, u32[32]{0:T(128)}, u32[]{:S(2)}) copy-start(u32[32]{0:T(128)} %constant.181) | copy-start | bytes 388
  7.2 7.8 copy-start.51
  7.2 8.9 %copy-start.52 = (s32[256]{0:T(256)S(1)}, s32[256]{0:T(256)}, u32[]{:S(2)}) copy-start(s32[256]{0:T(256)} %param.23) | copy-start | bytes 3076
  7.2 8.9 %copy-start.54 = (f32[16]{0:T(128)S(1)}, f32[16]{0:T(128)}, u32[]{:S(2)}) copy-start(f32[16]{0:T(128)} %param.21) | copy-start | bytes 196
  7.2 49.0 %copy-start.46 = (f32[16,1024]{1,0:T(8,128)S(1)}, f32[16,1024]{1,0:T(8,128)}, u32[]{:S(2)}) copy-start(f32[16,1024]{1,0:T(8,128)} %param.19) | copy-start | bytes 196612
  7.2 65.6 %all-gather.5.cloned.1.call-start = ((), (), s32[]{:S(2)}) async-start(), calls=%async_computation.2 | async-start | bytes 2973696 | tf_op jit(solution)/shard_map/all_gather | solution.py:1401
  8.9 116.0 %all-gather.9.cloned.1.call-start = ((), (), s32[]{:S(2)}) async-start(), calls=%async_computation.4 | async-start | bytes 4456448 | tf_op jit(solution)/shard_map/all_gather | solution.py:1397
  10.7 177.3 %all-gather.7.cloned.1.call-start = ((), (), s32[]{:S(2)}) async-start(), calls=%async_computation.3 | async-start | bytes 6684672 | tf_op jit(solution)/shard_map/all_gather | solution.py:1400
  12.7 45.7 %copy-start.47 = (f32[16,1024]{1,0:T(8,128)S(1)}, f32[16,1024]{1,0:T(8,128)}, u32[]{:S(2)}) copy-start(f32[16,1024]{1,0:T(8,128)} %param.20) | copy-start | bytes 196612
  12.7 308.5 %all-gather.11.cloned.1.call-start = ((), (), s32[]{:S(2)}) async-start(), calls=%async_computation.5 | async-start | bytes 8912896 | tf_op jit(solution)/shard_map/all_gather | solution.py:1398
  14.9 576.9 %reduce-scatter.3.cloned.1.call-start = ((), (), s32[]{:S(2)}) async-start(), calls=%async_computation.6 | async-start | bytes 4456448 | tf_op jit(solution)/shard_map/reduce_scatter | solution.py:1511
  61.8 140.0 %copy-start.1 = (f32[1024,256]{1,0:T(8,128)}, f32[1024,256]{1,0:T(8,128)S(1)}, u32[]{:S(2)}) copy-start(f32[1024,256]{1,0:T(8,128)S(1)} %copy.91.sin_ref) | copy-start | bytes 3145732
  62.2 139.6 %copy-start.2 = (f32[1024,256]{1,0:T(8,128)}, f32[1024,256]{1,0:T(8,128)S(1)}, u32[]{:S(2)}) copy-start(f32[1024,256]{1,0:T(8,128)S(1)} %copy.90.cos_ref) | copy-start | bytes 3145732
  62.3 234.9 %copy-start.4 = (s32[2]{0:T(128)}, s32[2]{0:T(128)S(1)}, u32[]{:S(2)}) copy-start(s32[2]{0:T(128)S(1)} %get-tuple-element.86.hi_ref) | copy-start | bytes 28
  62.3 234.9 %copy-start.5 = (s32[2]{0:T(128)}, s32[2]{0:T(128)S(1)}, u32[]{:S(2)}) copy-start(s32[2]{0:T(128)S(1)} %get-tuple-element.87.mid_ref) | copy-start | bytes 28
  62.3 234.9 %copy-start.6 = (s32[2]{0:T(128)}, s32[2]{0:T(128)S(1)}, u32[]{:S(2)}) copy-start(s32[2]{0:T(128)S(1)} %get-tuple-element.88.lo_ref) | copy-start | bytes 28
  62.8 15.2 %copy-start.35 = (f32[256,128]{1,0:T(8,128)}, f32[256,128]{1,0:T(8,128)S(1)}, u32[]{:S(2)}) copy-start(f32[256,128]{1,0:T(8,128)S(1)} %get-tuple-element.112) | copy-start | bytes 393220
  62.8 15.1 %copy-start.37 = (f32[256,128]{1,0:T(8,128)}, f32[256,128]{1,0:T(8,128)S(1)}, u32[]{:S(2)}) copy-start(f32[256,128]{1,0:T(8,128)S(1)} %get-tuple-element.113) | copy-start | bytes 393220
  188.1 13.7 %copy-start.7 = (bf16[256,256]{1,0:T(8,128)(2,1)S(1)}, bf16[256,256]{1,0:T(8,128)(2,1)}, u32[]{:S(2)}) copy-start(bf16[256,256]{1,0:T(8,128)(2,1)} %constant.160.clone.rot_ref) | copy-start | bytes 393220
  297.2 21.0 %copy-start.3 = (s32[8,1024]{1,0:T(8,128)}, s32[8,1024]{1,0:T(8,128)S(1)}, u32[]{:S(2)}) copy-start(s32[8,1024]{1,0:T(8,128)S(1)} %broadcast_in_dim.30.cs_ref) | copy-start | bytes 98308
  457.3 262.7 %reduce-scatter.5.cloned.1.call-start = ((), (), s32[]{:S(2)}) async-start(), calls=%async_computation.7 | async-start | bytes 5849088 | tf_op jit(solution)/shard_map/reduce_scatter | solution.py:1512
  469.7 35.1 %copy-start.44 = (f32[4,8,1024]{2,1,0:T(8,128)S(1)}, f32[4,8,1024]{2,1,0:T(8,128)}, u32[]{:S(2)}) copy-start(f32[4,8,1024]{2,1,0:T(8,128)} %get-tuple-element.64) | copy-start | bytes 393220
  591.8 127.5 %copy-start.39 = (bf16[64,2048]{1,0:T(8,128)(2,1)S(1)}, bf16[64,2048]{1,0:T(8,128)(2,1)}, u32[]{:S(2)}) copy-start(bf16[64,2048]{1,0:T(8,128)(2,1)} %reduce-scatter.3.cloned.1.call-done) | copy-start | bytes 786436
  722.7 96.6 %collective-permute-start = (f32[64,16]{1,0:T(8,128)S(1)}, f32[64,16]{1,0:T(8,128)S(1)}, u32[]{:S(2)}, u32[]{:S(2)}) collective-permute-start(f32[64,16]{1,0:T(8,128)S(1)} %slice.162), channel_id=1, source_target_pairs={{0,1},{1,0},{2,3},{3,2},{4,5},{5,4},{6,7},{7,6},{8,9},{9,8},{10,11... | collective-permute-start | bytes 12296 | tf_op jit(solution)/shard_map/ppermute | solution.py:1576
  (39 other events, 142.4 us)
Sparse Core Ops, SparseCore 0:
  11.5 61.2 all-gather.4
  75.6 49.2 all-gather.8
  127.7 60.3 all-gather.6
  190.7 102.2 all-gather.10
  457.5 134.2 reduce-scatter.2
  596.0 107.8 reduce-scatter.4
